TPU v7x, 512 devices: a whole 4x8x8 slice. The times are simulated.
512 devices in a mesh: pipe: 16 (over z, core), expert: 32 (over x, y).
Axes of the slice: x: 4, y: 8, z: 8, core: 2. Of those that a mesh axis runs over, the one named last changes fastest.
Arguments:
- section_acts: bfloat16 [16, 2048, 3584], P('pipe', 'expert'), may hold values from -6 to 6
- fwd_routes: int32 [16, 2048, 1], P('pipe', 'expert'), may hold values from 0 to 7; in each aligned block of 64 rows (0 to 63, 64 to 127, ..., all dimensions but the last counted through in order) at most 16 rows name the same one
- fwd_gates: float32 [16, 2048, 1], P('pipe', 'expert'), may hold values from 0.1 to 1
- section_grads: bfloat16 [16, 2048, 3584], P('pipe', 'expert'), may hold values from -6 to 6
- bwd_routes: int32 [16, 2048, 1], P('pipe', 'expert'), may hold values from 0 to 7; in each aligned block of 64 rows (0 to 63, 64 to 127, ..., all dimensions but the last counted through in order) at most 16 rows name the same one
- bwd_gates: float32 [16, 2048, 1], P('pipe', 'expert'), may hold values from 0.1 to 1
- saved_proj: bfloat16 [16, 32, 32, 16, 256], P('pipe', None, 'expert'), may hold values from -6 to 6
- w_gate: bfloat16 [16, 32, 3584, 128], P('pipe', 'expert'), may hold values from -0.09375 to 0.09375
- w_up: bfloat16 [16, 32, 3584, 128], P('pipe', 'expert'), may hold values from -0.09375 to 0.09375
- w_down: bfloat16 [16, 32, 128, 3584], P('pipe', 'expert'), may hold values from -0.1875 to 0.1875
Outputs:
- fwd_out: bfloat16 [16, 2048, 3584], P('pipe', 'expert')
- bwd_out: bfloat16 [16, 2048, 3584], P('pipe', 'expert')
- gate_grad: float32 [16, 2048, 1], P('pipe', 'expert')
Inputs may be any that keep to these rules, and one draw needn't show every extreme that they name: `fwd_routes`: in every section, among the 64 tokens of one index of expert no value is named by more than 16 of them, a bound that some block reaches.
All inputs are finite; a program needn't handle non-finite values.
Results may differ from a plain program's by a relative error of at most 0.009.
Values may be sent and summed in bfloat16 or wider, within the bound.
A program may use at most 64 MiB of HBM per device.

v0:
```python
import jax
import jax.numpy as jnp
from jax import lax
from jax.sharding import PartitionSpec as P

GROUP = 8


def passed_along(array, axis, by):
    length = lax.axis_size(axis)
    return lax.ppermute(array, axis, [(i, (i + by) % length) for i in range(length)])


def local_places(routes, experts, slots):
    expert_ids = jnp.arange(experts, dtype=jnp.int32)
    chosen = (routes[..., None] == expert_ids).astype(jnp.int32).sum(axis=1)
    before = jnp.cumsum(chosen, axis=0) - chosen
    clipped = jnp.clip(routes, 0, experts - 1)
    slot = jnp.take_along_axis(before, clipped, axis=1)
    place = clipped * slots + slot
    sentinel = jnp.full(place.shape, experts * slots, jnp.int32)
    return jnp.where(routes < experts, place, sentinel)


def pack_rows(values, place, experts, slots):
    count = values.shape[0]
    table = jnp.full((experts * slots + 1,), count, jnp.int32)
    owners = jnp.repeat(jnp.arange(count, dtype=jnp.int32), place.shape[1])
    table = table.at[place.reshape(-1)].set(owners)[:-1]
    padded = jnp.concatenate([values, jnp.zeros((1, values.shape[1]), values.dtype)], axis=0)
    packed = padded[table].reshape(experts, slots, values.shape[1])
    return jnp.repeat(packed, GROUP, axis=0)


def pack_gates(gates, place, experts, slots):
    buffer = (
        jnp.zeros((experts * slots + 1,), jnp.float32).at[place.reshape(-1)].set(gates.reshape(-1))
    )
    packed = buffer[:-1].reshape(experts, slots).astype(jnp.bfloat16)
    return jnp.repeat(packed, GROUP, axis=0)


def expert_forward(rows, weight_g, weight_u, weight_d):
    pre_g = jnp.einsum("sci,ih->sch", rows, weight_g, preferred_element_type=jnp.float32)
    pre_u = jnp.einsum("sci,ih->sch", rows, weight_u, preferred_element_type=jnp.float32)
    hidden = (pre_g * jax.nn.sigmoid(pre_g) * pre_u).astype(jnp.bfloat16)
    return jnp.einsum("sch,hi->sci", hidden, weight_d, preferred_element_type=jnp.float32).astype(
        jnp.bfloat16
    )


def expert_backward(rows, gate_rows, kept, weight_g, weight_u, weight_d):
    width = weight_g.shape[1]
    sg = kept[..., :width].astype(jnp.float32)
    su = kept[..., width:].astype(jnp.float32)
    sig = jax.nn.sigmoid(sg)
    act = sg * sig
    hidden = (act * su).astype(jnp.bfloat16)
    out_rows = jnp.einsum("sch,hi->sci", hidden, weight_d, preferred_element_type=jnp.float32)
    rows_wide = rows.astype(jnp.float32)
    slot_part = jnp.sum(rows_wide * out_rows, axis=-1).astype(jnp.bfloat16)
    scaled = (gate_rows.astype(jnp.float32)[..., None] * rows_wide).astype(jnp.bfloat16)
    dhid = jnp.einsum("sci,hi->sch", scaled, weight_d, preferred_element_type=jnp.float32)
    d_gate = (dhid * su * sig * (1.0 + sg * (1.0 - sig))).astype(jnp.bfloat16)
    d_upper = (dhid * act).astype(jnp.bfloat16)
    dx_part = jnp.einsum("sch,ih->sci", d_gate, weight_g, preferred_element_type=jnp.float32)
    dx_part = dx_part + jnp.einsum(
        "sch,ih->sci", d_upper, weight_u, preferred_element_type=jnp.float32
    )
    return (dx_part.astype(jnp.bfloat16), slot_part)


def fold_shards(buffer, experts):
    shaped = buffer.reshape((experts, GROUP) + buffer.shape[1:])
    return jnp.sum(shaped.astype(jnp.float32), axis=1)


def unpack_rows(folded, place):
    flat = folded.reshape(-1, folded.shape[-1])
    padded = jnp.concatenate([flat, jnp.zeros((1, flat.shape[1]), flat.dtype)], axis=0)
    return padded[place]


def on_device(
    section_acts,
    fwd_routes,
    fwd_gates,
    section_grads,
    bwd_routes,
    bwd_gates,
    saved_proj,
    w_gate,
    w_up,
    w_down,
):
    experts = lax.axis_size("expert") // GROUP
    slots = saved_proj.shape[3]
    inputs = passed_along(section_acts, "pipe", 1)[0]
    cotan = passed_along(section_grads, "pipe", -1)[0]
    weight_g = w_gate[0, 0]
    weight_u = w_up[0, 0]
    weight_d = w_down[0, 0]
    kept = saved_proj[0, :, 0]
    place_a = local_places(fwd_routes[0], experts, slots)
    place_b = local_places(bwd_routes[0], experts, slots)
    rows_a = pack_rows(inputs, place_a, experts, slots)
    rows_b = pack_rows(cotan, place_b, experts, slots)
    gate_b = pack_gates(bwd_gates[0], place_b, experts, slots)
    result = expert_forward(
        lax.all_to_all(rows_a, "expert", split_axis=0, concat_axis=0, tiled=True),
        weight_g,
        weight_u,
        weight_d,
    )
    back_a = lax.all_to_all(result, "expert", split_axis=0, concat_axis=0, tiled=True)
    recv_b, recv_g = (
        lax.all_to_all(rows_b, "expert", split_axis=0, concat_axis=0, tiled=True),
        lax.all_to_all(gate_b, "expert", split_axis=0, concat_axis=0, tiled=True),
    )
    dx_part, slot_part = expert_backward(recv_b, recv_g, kept, weight_g, weight_u, weight_d)
    back_b, back_g = (
        lax.all_to_all(dx_part, "expert", split_axis=0, concat_axis=0, tiled=True),
        lax.all_to_all(slot_part, "expert", split_axis=0, concat_axis=0, tiled=True),
    )
    picked_a = unpack_rows(fold_shards(back_a, experts), place_a)
    total_a = inputs.astype(jnp.float32) + jnp.sum(fwd_gates[0][..., None] * picked_a, axis=1)
    picked_b = unpack_rows(fold_shards(back_b, experts), place_b)
    total_b = cotan.astype(jnp.float32) + jnp.sum(picked_b, axis=1)
    slot_sum = fold_shards(back_g, experts).reshape(-1)
    grads = jnp.concatenate([slot_sum, jnp.zeros((1,), jnp.float32)])[place_b]
    return (total_a.astype(jnp.bfloat16)[None], total_b.astype(jnp.bfloat16)[None], grads[None])


def solution(mesh):
    placed = (
        P("pipe", "expert", None),
        P("pipe", "expert", None),
        P("pipe", "expert", None),
        P("pipe", "expert", None),
        P("pipe", "expert", None),
        P("pipe", "expert", None),
        P("pipe", None, "expert", None, None),
        P("pipe", "expert", None, None),
        P("pipe", "expert", None, None),
        P("pipe", "expert", None, None),
    )
    return jax.shard_map(
        on_device,
        mesh=mesh,
        in_specs=placed,
        out_specs=(P("pipe", "expert", None), P("pipe", "expert", None), P("pipe", "expert", None)),
        check_vma=False,
    )
```

profile of v0, /device:TPU:192, one launch (start us, length us, event | category | flops | bytes accessed | tf_op | source)
XLA Modules:
  0.0 424.7 jit_solution(10468802521737029754)
XLA Ops:
  0.7 0.7 fusion.59
  1.4 0.7 fusion.60
  2.1 0.7 fusion.40
  2.8 0.1 reduce_window_sum.18
  2.9 0.7 fusion.41
  3.7 0.8 gather_fusion.6
  4.5 0.7 fusion.48
  5.1 0.8 scatter_custom_fusion.2
  6.0 1.0 collective-permute-done.1
  7.0 0.8 gather_fusion.2
  7.8 2.3 broadcast_in_dim.45
  10.1 10.2 %all-to-all-start.3 = ((bf16[32,16,3584]{2,1,0:T(8,128)(2,1)}), bf16[32,16,3584]{2,1,0:T(8,128)(2,1)}, u32[]{:S(2)}, u32[]{:S(2)}) async-start(bf16[32,16,3584]{2,1,0:T(8,128)(2,1)} %bitcast.135), calls=%async_computation.3 | async-start | bytes 7340032 | tf_op jit(solution)/shard_map/all_to_all | solution.py:117
  20.3 3.5 collective-permute-start
  23.9 0.1 reduce_window_sum.17
  24.1 0.8 gather_fusion.5
  24.9 0.8 scatter_custom_fusion
  25.7 2.5 collective-permute-done
  28.2 0.8 copy-done.3
  29.0 0.8 gather_fusion
  29.9 76.6 %all-to-all-done.3 = bf16[32,16,3584]{2,1,0:T(8,128)(2,1)} async-done(((bf16[32,16,3584]{2,1,0:T(8,128)(2,1)}), bf16[32,16,3584]{2,1,0:T(8,128)(2,1)}, u32[]{:S(2)}, u32[]{:S(2)}) %all-to-all-start.3) | async-done | bytes 3670048 | tf_op jit(solution)/shard_map/all_to_all | solution.py:117
  106.4 2.3 broadcast_in_dim.40
  108.7 5.8 %all-to-all-start = ((bf16[32,16,3584]{2,1,0:T(8,128)(2,1)}), bf16[32,16,3584]{2,1,0:T(8,128)(2,1)}, u32[]{:S(2)}, u32[]{:S(2)}) async-start(bf16[32,16,3584]{2,1,0:T(8,128)(2,1)} %bitcast.136), calls=%async_computation | async-start | bytes 7340032 | tf_op jit(solution)/shard_map/all_to_all | solution.py:110
  114.5 1.0 scatter_custom_fusion.1
  115.6 0.6 copy.18
  116.2 3.4 fusion.1
  119.6 80.1 %all-to-all-done = bf16[32,16,3584]{2,1,0:T(8,128)(2,1)} async-done(((bf16[32,16,3584]{2,1,0:T(8,128)(2,1)}), bf16[32,16,3584]{2,1,0:T(8,128)(2,1)}, u32[]{:S(2)}, u32[]{:S(2)}) %all-to-all-start) | async-done | bytes 3670048 | tf_op jit(solution)/shard_map/all_to_all | solution.py:110
  199.7 7.6 %all-to-all-start.2 = ((bf16[32,1,16]{2,1,0:T(2,128)(2,1)}), bf16[32,1,16]{2,1,0:T(2,128)(2,1)S(1)}, u32[]{:S(2)}, u32[]{:S(2)}) async-start(bf16[32,1,16]{2,1,0:T(2,128)(2,1)} %copy.18), calls=%async_computation.2 | async-start | bytes 32768 | tf_op jit(solution)/shard_map/all_to_all | solution.py:118
  207.3 3.1 fusion.12
  210.6 0.7 copy.20
  211.3 5.8 %all-to-all-done.2 = bf16[32,1,16]{2,1,0:T(2,128)(2,1)S(1)} async-done(((bf16[32,1,16]{2,1,0:T(2,128)(2,1)}), bf16[32,1,16]{2,1,0:T(2,128)(2,1)S(1)}, u32[]{:S(2)}, u32[]{:S(2)}) %all-to-all-start.2) | async-done | bytes 1056 | tf_op jit(solution)/shard_map/all_to_all | solution.py:118
  217.0 4.0 all-to-all-start.5
  221.1 8.1 %convolution_convert_fusion = bf16[32,16,3584]{2,1,0:T(8,128)(2,1)} fusion(bf16[32,16,3584]{2,1,0:T(8,128)(2,1)} %all-to-all-done, bf16[1,1,3584,128]{3,2,1,0:T(8,128)(2,1)S(1)} %copy-done, bf16[1,1,128,3584]{3,2,1,0:T(8,128)(2,1)} %param.21, f32[32,16,128]{2,1,0:T(8,128)S(1)} %fusion.12), kind=kOutput, calls=%fused_computation.17 | convolution fusion | flops 941752320 | bytes 9437184 | tf_op jit(solution)/shard_map/sch,hi->sci/dot_general | solution.py:47
  229.1 1.7 all-to-all-done.5
  230.8 8.4 %all-to-all-start.1 = ((bf16[32,16,3584]{2,1,0:T(8,128)(2,1)}), bf16[32,16,3584]{2,1,0:T(8,128)(2,1)}, u32[]{:S(2)}, u32[]{:S(2)}) async-start(bf16[32,16,3584]{2,1,0:T(8,128)(2,1)} %convolution_convert_fusion), calls=%async_computation.1 | async-start | bytes 7340032 | tf_op jit(solution)/shard_map/all_to_all | solution.py:115
  239.3 3.5 fusion.2
  242.8 1.1 fusion.10
  243.9 2.9 add_convert_fusion
  246.8 77.3 %all-to-all-done.1 = bf16[32,16,3584]{2,1,0:T(8,128)(2,1)} async-done(((bf16[32,16,3584]{2,1,0:T(8,128)(2,1)}), bf16[32,16,3584]{2,1,0:T(8,128)(2,1)}, u32[]{:S(2)}, u32[]{:S(2)}) %all-to-all-start.1) | async-done | bytes 3670048 | tf_op jit(solution)/shard_map/all_to_all | solution.py:115
  324.1 6.1 %all-to-all-start.4 = ((bf16[32,16,3584]{2,1,0:T(8,128)(2,1)}), bf16[32,16,3584]{2,1,0:T(8,128)(2,1)}, u32[]{:S(2)}, u32[]{:S(2)}) async-start(bf16[32,16,3584]{2,1,0:T(8,128)(2,1)} %add_convert_fusion), calls=%async_computation.4 | async-start | bytes 7340032 | tf_op jit(solution)/shard_map/all_to_all | solution.py:122
  330.3 0.1 reshape.240
  330.5 1.3 gather_fusion.4
  331.8 2.6 convert_reduce_fusion.1
  334.5 80.8 %all-to-all-done.4 = bf16[32,16,3584]{2,1,0:T(8,128)(2,1)} async-done(((bf16[32,16,3584]{2,1,0:T(8,128)(2,1)}), bf16[32,16,3584]{2,1,0:T(8,128)(2,1)}, u32[]{:S(2)}, u32[]{:S(2)}) %all-to-all-start.4) | async-done | bytes 3670048 | tf_op jit(solution)/shard_map/all_to_all | solution.py:122
  415.3 2.6 convert_reduce_fusion
  418.0 1.8 gather_fusion.3
  419.8 1.8 gather_fusion.1
  421.6 0.8 fusion.6
  422.5 2.2 fusion.18
  (44 shorter events, 0.8 us)
Async XLA Ops:
  0.6 220.4 %copy-start = (bf16[1,1,3584,128]{3,2,1,0:T(8,128)(2,1)S(1)}, bf16[1,1,3584,128]{3,2,1,0:T(8,128)(2,1)}, u32[]{:S(2)}) copy-start(bf16[1,1,3584,128]{3,2,1,0:T(8,128)(2,1)} %param.20) | copy-start | bytes 2752516
  0.6 6.3 %collective-permute-start.1 = (bf16[1,64,3584]{2,1,0:T(8,128)(2,1)}, bf16[1,64,3584]{2,1,0:T(8,128)(2,1)S(1)}, u32[]{:S(2)}, u32[]{:S(2)}) collective-permute-start(bf16[1,64,3584]{2,1,0:T(8,128)(2,1)} %param.15), channel_id=1, source_target_pairs={{0,480},{32,0},{64,32},{96,64},{128,96},{160,128},{192,160},{224,1... | collective-permute-start | bytes 1376264 | tf_op jit(solution)/shard_map/ppermute | solution.py:11
  10.1 10.2 %copy-start.8 = (bf16[1,64,3584]{2,1,0:T(8,128)(2,1)S(1)}, bf16[1,64,3584]{2,1,0:T(8,128)(2,1)}, u32[]{:S(2)}) copy-start(bf16[1,64,3584]{2,1,0:T(8,128)(2,1)} %param.12) | copy-start | bytes 1376260
  10.1 13.7 %copy-start.6 = (s32[1,64,1]{1,2,0:T(1,128)S(1)}, s32[1,64,1]{1,2,0:T(1,128)}, u32[]{:S(2)}) copy-start(s32[1,64,1]{1,2,0:T(1,128)} %param.13) | copy-start | bytes 772
  10.1 96.3 %all-to-all-start.3 = ((bf16[32,16,3584]{2,1,0:T(8,128)(2,1)}), bf16[32,16,3584]{2,1,0:T(8,128)(2,1)}, u32[]{:S(2)}, u32[]{:S(2)}) async-start(bf16[32,16,3584]{2,1,0:T(8,128)(2,1)} %bitcast.135), calls=%async_computation.3 | async-start | bytes 7340032 | tf_op jit(solution)/shard_map/all_to_all | solution.py:117
  20.3 7.9 %collective-permute-start = (bf16[1,64,3584]{2,1,0:T(8,128)(2,1)S(1)}, bf16[1,64,3584]{2,1,0:T(8,128)(2,1)S(1)}, u32[]{:S(2)}, u32[]{:S(2)}) collective-permute-start(bf16[1,64,3584]{2,1,0:T(8,128)(2,1)S(1)} %copy-done.8), channel_id=1, source_target_pairs={{0,32},{32,64},{64,96},{96,128},{128,160},{160,192},{192,224},{224... | collective-permute-start | bytes 1376264 | tf_op jit(solution)/shard_map/ppermute | solution.py:11
  28.2 0.8 copy-start.3
  108.7 7.6 %copy-start.4 = (bf16[1,1,128,3584]{3,2,1,0:T(8,128)(2,1)S(1)}, bf16[1,1,128,3584]{3,2,1,0:T(8,128)(2,1)}, u32[]{:S(2)}) copy-start(bf16[1,1,128,3584]{3,2,1,0:T(8,128)(2,1)} %param.21) | copy-start | bytes 2752516
  108.7 91.0 %all-to-all-start = ((bf16[32,16,3584]{2,1,0:T(8,128)(2,1)}), bf16[32,16,3584]{2,1,0:T(8,128)(2,1)}, u32[]{:S(2)}, u32[]{:S(2)}) async-start(bf16[32,16,3584]{2,1,0:T(8,128)(2,1)} %bitcast.136), calls=%async_computation | async-start | bytes 7340032 | tf_op jit(solution)/shard_map/all_to_all | solution.py:110
  114.5 92.9 %copy-start.1 = (bf16[1,1,3584,128]{3,2,1,0:T(8,128)(2,1)S(1)}, bf16[1,1,3584,128]{3,2,1,0:T(8,128)(2,1)}, u32[]{:S(2)}) copy-start(bf16[1,1,3584,128]{3,2,1,0:T(8,128)(2,1)} %param.19) | copy-start | bytes 2752516
  199.7 17.3 %all-to-all-start.2 = ((bf16[32,1,16]{2,1,0:T(2,128)(2,1)}), bf16[32,1,16]{2,1,0:T(2,128)(2,1)S(1)}, u32[]{:S(2)}, u32[]{:S(2)}) async-start(bf16[32,1,16]{2,1,0:T(2,128)(2,1)} %copy.18), calls=%async_computation.2 | async-start | bytes 32768 | tf_op jit(solution)/shard_map/all_to_all | solution.py:118
  217.0 13.8 %all-to-all-start.5 = ((bf16[32,1,16]{2,1,0:T(2,128)(2,1)}), bf16[32,1,16]{2,1,0:T(2,128)(2,1)S(1)}, u32[]{:S(2)}, u32[]{:S(2)}) async-start(bf16[32,1,16]{2,1,0:T(2,128)(2,1)} %copy.20), calls=%async_computation.5 | async-start | bytes 32768 | tf_op jit(solution)/shard_map/all_to_all | solution.py:123
  230.8 93.3 %all-to-all-start.1 = ((bf16[32,16,3584]{2,1,0:T(8,128)(2,1)}), bf16[32,16,3584]{2,1,0:T(8,128)(2,1)}, u32[]{:S(2)}, u32[]{:S(2)}) async-start(bf16[32,16,3584]{2,1,0:T(8,128)(2,1)} %convolution_convert_fusion), calls=%async_computation.1 | async-start | bytes 7340032 | tf_op jit(solution)/shard_map/all_to_all | solution.py:115
  239.2 3.5 copy-start.5
  324.1 91.2 %all-to-all-start.4 = ((bf16[32,16,3584]{2,1,0:T(8,128)(2,1)}), bf16[32,16,3584]{2,1,0:T(8,128)(2,1)}, u32[]{:S(2)}, u32[]{:S(2)}) async-start(bf16[32,16,3584]{2,1,0:T(8,128)(2,1)} %add_convert_fusion), calls=%async_computation.4 | async-start | bytes 7340032 | tf_op jit(solution)/shard_map/all_to_all | solution.py:122
  419.8 1.8 copy-start.2
  419.8 2.6 copy-start.7
where the time goes:
time: 425 us
  waiting for transfers between devices  326 us (77%)
  starting transfers between devices  45.6 us (11%)
  matrix products  22.1 us (5%)
  local copies, waits for them, and re-layouts  17.9 us (4%)
  other arithmetic  12.4 us (3%)
    all_to_all x1, waiting for transfers between devices, on_device(): lax.all_to_all(dx_part, 'expert', split_axis=0, concat_axis=0, tiled=True)  80.8 us
    all_to_all x1, waiting for transfers between devices, on_device(): lax.all_to_all(rows_a, 'expert', split_axis=0, concat_axis=0, tiled=True)  80.1 us
    all_to_all x1, waiting for transfers between devices, on_device(): lax.all_to_all(result, 'expert', split_axis=0, concat_axis=0, tiled=True)  77.3 us
    all_to_all x1, waiting for transfers between devices, on_device(): lax.all_to_all(rows_b, 'expert', split_axis=0, concat_axis=0, tiled=True)  76.6 us
    all_to_all x1, starting transfers between devices, on_device(): lax.all_to_all(rows_b, 'expert', split_axis=0, concat_axis=0, tiled=True)  10.2 us
  transfers between devices with their start and end apart: 8, of which 8 were waited for; matrix products, arithmetic and copies ran while one was open for 9% of the time, Pallas kernels for 0%

commit v1 on v0

v1 whole, which is shorter than its diff:
```python
import functools

import jax
import jax.numpy as jnp
from jax import lax
from jax.experimental import pallas as pl
from jax.experimental.pallas import tpu as pltpu
from jax.sharding import PartitionSpec as P

GROUP = 8
CHUNKS = 4
PAIRS = GROUP // 2
HOPS = 4
MESH = pl.DeviceIdType.MESH
WAYS = ((0, 1), (1, -1))
f32 = jnp.float32
bf16 = jnp.bfloat16


def nt_dot(a, b):
    return lax.dot_general(a, b, (((1,), (1,)), ((), ())), preferred_element_type=f32)


def column_of(row):
    count = row.shape[1]
    shape = (count, count)
    eye = lax.broadcasted_iota(jnp.int32, shape, 0) == lax.broadcasted_iota(jnp.int32, shape, 1)
    return jnp.sum(jnp.where(eye, jnp.broadcast_to(row, shape), 0.0), axis=1, keepdims=True)


def row_of(column):
    count = column.shape[0]
    shape = (count, count)
    eye = lax.broadcasted_iota(jnp.int32, shape, 0) == lax.broadcasted_iota(jnp.int32, shape, 1)
    return jnp.sum(jnp.where(eye, jnp.broadcast_to(column, shape), 0.0), axis=0, keepdims=True)


def place_matrices(route_row, experts, cap):
    tokens = route_row.shape[1]
    slots = experts * cap
    routes = route_row.astype(f32)
    column = column_of(routes)
    at = lax.broadcasted_iota(jnp.int32, (tokens, tokens), 0)
    other = lax.broadcasted_iota(jnp.int32, (tokens, tokens), 1)
    slot = lax.broadcasted_iota(jnp.int32, (slots, tokens), 0)
    named = jnp.broadcast_to(routes, (slots, tokens)) == (slot // cap).astype(f32)
    before = jnp.dot(
        jnp.where(named, 1.0, 0.0).astype(bf16),
        jnp.where(at < other, 1.0, 0.0).astype(bf16),
        preferred_element_type=f32,
    )
    pack = jnp.where(named & (before == (slot % cap).astype(f32)), 1.0, 0.0).astype(bf16)
    slot = lax.broadcasted_iota(jnp.int32, (tokens, slots), 1)
    named = jnp.broadcast_to(column, (tokens, slots)) == (slot // cap).astype(f32)
    before = jnp.dot(
        jnp.where(other < at, 1.0, 0.0).astype(bf16),
        jnp.where(named, 1.0, 0.0).astype(bf16),
        preferred_element_type=f32,
    )
    unpack = jnp.where(named & (before == (slot % cap).astype(f32)), 1.0, 0.0).astype(bf16)
    return pack, unpack


def kernel(
    acts,
    grads,
    routes_a,
    gates_a,
    routes_b,
    gates_b,
    kept,
    w_gate,
    w_up,
    w_down,
    out_a,
    out_b,
    out_g,
    in_a,
    in_b,
    packed_a,
    packed_b,
    rows_a,
    rows_b,
    part_a,
    part_b,
    sums_a,
    sums_b,
    back_a,
    back_b,
    whole_a,
    whole_b,
    wide,
    down,
    saved,
    slot_own,
    slot_sent,
    slot_got,
    slot_fold,
    slot_back,
    load_sem,
    save_sem,
    pipe_send,
    pipe_recv,
    spread_send,
    spread_recv,
    ring_send,
    ring_recv,
    fold_send,
    fold_recv,
    home_send,
    home_recv,
    slot_send,
    slot_recv,
    last_send,
    last_recv,
):
    stage = lax.axis_index("pipe")
    stages = lax.axis_size("pipe")
    index = lax.axis_index("expert")
    x = index // GROUP
    y = index % GROUP
    chunks, experts, cap, width = packed_a.shape
    hidden = down.shape[1]
    half = experts // 2
    spread = experts * cap

    def column(xx):
        return {"expert": xx * GROUP + y}

    def ring(by):
        return {"expert": x * GROUP + (y + GROUP + by) % GROUP}

    def along(by):
        return {"pipe": (stage + stages + by) % stages}

    def remote(src, dst, send, recv, device):
        return pltpu.make_async_remote_copy(
            src_ref=src,
            dst_ref=dst,
            send_sem=send,
            recv_sem=recv,
            device_id=device,
            device_id_type=MESH,
        )

    def start_of(c):
        return c * width if isinstance(c, int) else pl.multiple_of(c * width, 128)

    def each_chunk(body):
        lax.fori_loop(0, chunks, lambda c, carry: (body(c), carry)[1], 0)

    loads = [
        pltpu.make_async_copy(w_gate.at[0, 0], wide.at[:, pl.ds(0, hidden)], load_sem.at[0]),
        pltpu.make_async_copy(w_up.at[0, 0], wide.at[:, pl.ds(hidden, hidden)], load_sem.at[1]),
        pltpu.make_async_copy(kept.at[0, :, 0], saved, load_sem.at[2]),
    ]
    for c in range(chunks):
        loads.append(
            pltpu.make_async_copy(
                w_down.at[0, 0, :, pl.ds(c * width, width)], down.at[c], load_sem.at[3 + c]
            )
        )

    barrier = pltpu.get_barrier_semaphore()
    partners = [along(1), along(-1), ring(1), ring(-1)]
    partners += [column((x + j) % experts) for j in range(1, experts)]
    for partner in partners:
        pl.semaphore_signal(barrier, inc=1, device_id=partner, device_id_type=MESH)
    pl.semaphore_wait(barrier, len(partners))

    def pipe_copy(ab, c):
        source, target = ((acts, in_a), (grads, in_b))[ab]
        return remote(
            source.at[0, :, pl.ds(start_of(c), width)],
            target.at[c],
            pipe_send.at[ab, c],
            pipe_recv.at[ab, c],
            along(1 - 2 * ab),
        )

    for ab in (0, 1):
        for c in range(chunks):
            pipe_copy(ab, c).start()
    for load in loads:
        load.start()

    pack_a, unpack_a = place_matrices(routes_a[...], experts, cap)
    pack_b, unpack_b = place_matrices(routes_b[...], experts, cap)
    gate_a = column_of(gates_a[...])
    gate_b = column_of(gates_b[...].astype(bf16).astype(f32))

    def spread_copy(ab, c, j):
        packed, rows = ((packed_a, rows_a), (packed_b, rows_b))[ab]
        to = (x + j) % experts
        return remote(
            packed.at[c, to],
            rows.at[y, c, x],
            spread_send.at[ab, c, j - 1],
            spread_recv.at[ab, c, j - 1],
            column(to),
        )

    def pack_chunk(ab, c):
        source, packed, rows = ((in_a, packed_a, rows_a), (in_b, packed_b, rows_b))[ab]
        pack = (pack_a, pack_b)[ab]
        remote(
            source.at[c], source.at[c], pipe_send.at[ab, c], pipe_recv.at[ab, c], along(1)
        ).wait_recv()
        chosen = jnp.dot(pack, source[c], preferred_element_type=f32).astype(bf16)
        packed[c] = chosen.reshape(experts, cap, width)
        for j in range(1, experts):
            spread_copy(ab, c, j).start()
        rows[y, c, x] = packed[c, x]

    def spread_wait(ab, c):
        rows = (rows_a, rows_b)[ab]
        for j in range(1, experts):
            got = rows.at[y, c, (x + experts - j) % experts]
            remote(
                got, got, spread_send.at[ab, c, j - 1], spread_recv.at[ab, c, j - 1], column(x)
            ).wait_recv()

    def halves(ref, d, t, far):
        return ref.at[pl.ds(d * half, half)] if t == far else ref

    def ring_copy(ab, t, c, d, sign):
        rows = (rows_a, rows_b)[ab]
        block = halves(rows.at[(y + GROUP - sign * t) % GROUP, c], d, t, HOPS - 1)
        return remote(
            block,
            block,
            ring_send.at[ab, d, t * chunks + c],
            ring_recv.at[ab, d, t * chunks + c],
            ring(sign),
        )

    def ring_wait(ab, t, c, d, sign):
        rows = (rows_a, rows_b)[ab]
        block = halves(rows.at[(y + GROUP - sign * (t + 1)) % GROUP, c], d, t, HOPS - 1)
        remote(
            block,
            block,
            ring_send.at[ab, d, t * chunks + c],
            ring_recv.at[ab, d, t * chunks + c],
            ring(sign),
        ).wait_recv()

    def ring_step(ab, t, c):
        for d, sign in WAYS:
            if t:
                ring_wait(ab, t - 1, c, d, sign)
            ring_copy(ab, t, c, d, sign).start()

    def ring_last(ab, c):
        for d, sign in WAYS:
            ring_wait(ab, HOPS - 1, c, d, sign)

    def fold_copy(ab, t, c, d, sign):
        part, sums = ((part_a, sums_a), (part_b, sums_b))[ab]
        block = part.at[(y + GROUP + sign * (HOPS - t)) % GROUP, c]
        return remote(
            halves(block, d, t, 0),
            halves(sums.at[d, t, c], d, t, 0),
            fold_send.at[ab, d, t * chunks + c],
            fold_recv.at[ab, d, t * chunks + c],
            ring(sign),
        )

    def fold_wait(ab, t, c, d, sign):
        sums = (sums_a, sums_b)[ab]
        got = halves(sums.at[d, t, c], d, t, 0)
        remote(
            got,
            got,
            fold_send.at[ab, d, t * chunks + c],
            fold_recv.at[ab, d, t * chunks + c],
            ring(sign),
        ).wait_recv()

    def fold_step(ab, t, c):
        part, sums = ((part_a, sums_a), (part_b, sums_b))[ab]
        for d, sign in WAYS:
            block = (y + GROUP + sign * (HOPS - t)) % GROUP
            if t:
                fold_wait(ab, t - 1, c, d, sign)
                at = pl.ds(d * half, half) if t == 1 else pl.ds(0, experts)
                part[block, c, at] = (
                    part[block, c, at].astype(f32) + sums[d, t - 1, c, at].astype(f32)
                ).astype(bf16)
            fold_copy(ab, t, c, d, sign).start()

    def home_copy(ab, c, j):
        part, back = ((part_a, back_a), (part_b, back_b))[ab]
        to = (x + j) % experts
        return remote(
            part.at[y, c, to],
            back.at[c, x],
            home_send.at[ab, c, j - 1],
            home_recv.at[ab, c, j - 1],
            column(to),
        )

    def fold_last(ab, c):
        part, sums, back = ((part_a, sums_a, back_a), (part_b, sums_b, back_b))[ab]
        for d, sign in WAYS:
            fold_wait(ab, HOPS - 1, c, d, sign)
        part[y, c] = (
            part[y, c].astype(f32)
            + sums[0, HOPS - 1, c].astype(f32)
            + sums[1, HOPS - 1, c].astype(f32)
        ).astype(bf16)
        for j in range(1, experts):
            home_copy(ab, c, j).start()
        back[c, x] = part[y, c, x]

    def save_copy(ab, c):
        whole, out = ((whole_a, out_a), (whole_b, out_b))[ab]
        return pltpu.make_async_copy(
            whole.at[c], out.at[0, :, pl.ds(start_of(c), width)], save_sem.at[ab, c]
        )

    def finish(ab, c):
        source, back, whole = ((in_a, back_a, whole_a), (in_b, back_b, whole_b))[ab]
        unpack, gate = ((unpack_a, gate_a), (unpack_b, gate_b))[ab]
        for j in range(1, experts):
            got = back.at[c, (x + experts - j) % experts]
            remote(
                got, got, home_send.at[ab, c, j - 1], home_recv.at[ab, c, j - 1], column(x)
            ).wait_recv()
        picked = jnp.dot(unpack, back[c].reshape(spread, width), preferred_element_type=f32)
        whole[c] = (source[c].astype(f32) + gate * picked).astype(bf16)
        save_copy(ab, c).start()

    def pair_rows(rows, p, c):
        return rows[pl.ds(2 * p, 2), c].reshape(2 * spread, width)

    def forward(p):
        pre = jnp.zeros((2 * spread, 2 * hidden), f32)
        for c in range(chunks):
            pre += jnp.dot(
                pair_rows(rows_a, p, c),
                wide[pl.ds(c * width, width), :],
                preferred_element_type=f32,
            )
        pre_g, pre_u = pre[:, :hidden], pre[:, hidden:]
        hid = (pre_g * jax.nn.sigmoid(pre_g) * pre_u).astype(bf16)
        for c in range(chunks):
            part_a[pl.ds(2 * p, 2), c] = (
                jnp.dot(hid, down[c], preferred_element_type=f32)
                .astype(bf16)
                .reshape(2, experts, cap, width)
            )

    def backward(p):
        dhid = jnp.zeros((2 * spread, hidden), f32)
        for c in range(chunks):
            dhid += nt_dot(pair_rows(rows_b, p, c), down[c])
        both = jnp.concatenate(
            [saved[j * GROUP + 2 * p + i] for i in (0, 1) for j in range(experts)], axis=0
        ).astype(f32)
        sg, su = both[:, :hidden], both[:, hidden:]
        sig = jax.nn.sigmoid(sg)
        act = sg * sig
        hid = (act * su).astype(bf16).astype(f32)
        slot_row = jnp.sum((hid * dhid).T, axis=0, keepdims=True)
        slot_own[p] = jnp.broadcast_to(slot_row, slot_own.shape[1:])
        d_g = (dhid * su * sig * (1.0 + sg * (1.0 - sig))).astype(bf16)
        d_u = (dhid * act).astype(bf16)
        d_both = jnp.concatenate([d_g, d_u], axis=1)
        for c in range(chunks):
            part_b[pl.ds(2 * p, 2), c] = (
                nt_dot(d_both, wide[pl.ds(c * width, width), :])
                .astype(bf16)
                .reshape(2, experts, cap, width)
            )

    def slot_copy(d, t, sign):
        return remote(
            slot_sent.at[d, t],
            slot_got.at[d, t],
            slot_send.at[d, t],
            slot_recv.at[d, t],
            ring(sign),
        )

    def slot_step(t):
        for d, sign in WAYS:
            if t < d:
                continue
            pair = ((y + GROUP + sign * (HOPS - t)) % GROUP) // 2
            if t > d:
                slot_copy(d, t - 1, sign).wait_recv()
                slot_sent[d, t] = slot_own[pair] + slot_got[d, t - 1]
            else:
                slot_sent[d, t] = slot_own[pair]
            slot_copy(d, t, sign).start()

    def last_copy(j):
        return remote(
            slot_fold,
            slot_back.at[x],
            last_send.at[j - 1],
            last_recv.at[j - 1],
            column((x + j) % experts),
        )

    def slot_last():
        for d, sign in WAYS:
            slot_copy(d, HOPS - 1, sign).wait_recv()
        slot_fold[...] = slot_own[y // 2] + slot_got[0, HOPS - 1] + slot_got[1, HOPS - 1]
        for j in range(1, experts):
            last_copy(j).start()
        slot_back[x] = slot_fold[...]

    def slot_finish():
        for j in range(1, experts):
            got = slot_back.at[(x + experts - j) % experts]
            remote(
                got, got, last_send.at[j - 1], last_recv.at[j - 1], column(x)
            ).wait_recv()
        tokens = routes_b.shape[1]
        lanes = slot_back.shape[2]
        routes = column_of(routes_b[...].astype(f32))
        lane = lax.broadcasted_iota(jnp.int32, (tokens, spread), 1)
        taken = jnp.where(unpack_b > 0, (lane % cap).astype(f32), 0.0)
        slot = jnp.sum(taken, axis=1, keepdims=True)
        lane = lax.broadcasted_iota(jnp.int32, (tokens, lanes), 1)
        first = (y % 2) * spread + x * cap
        here = jnp.broadcast_to(slot, (tokens, lanes)) == (lane - first).astype(f32)
        total = jnp.zeros((tokens, lanes), f32)
        for e in range(experts):
            values = jnp.broadcast_to(slot_back[e][0:1], (tokens, lanes))
            total += jnp.where(here & (routes == float(e)), values, 0.0)
        out_g[...] = row_of(jnp.sum(total, axis=1, keepdims=True))

    for c in range(chunks):
        pack_chunk(0, c)
        if c:
            spread_wait(0, c - 1)
            ring_step(0, 0, c - 1)
    spread_wait(0, chunks - 1)
    ring_step(0, 0, chunks - 1)

    def body(c):
        ring_step(0, 1, c)
        pack_chunk(1, c)

    each_chunk(body)

    def body(c):
        ring_step(0, 2, c)
        spread_wait(1, c)

    each_chunk(body)
    each_chunk(lambda c: ring_step(0, 3, c))

    each_chunk(lambda c: ring_step(1, 0, c))
    each_chunk(lambda c: ring_last(0, c))
    for load in loads:
        load.wait()

    def body(c):
        ring_step(1, 1, c)
        forward(c)

    each_chunk(body)
    each_chunk(lambda c: ring_step(1, 2, c))
    each_chunk(lambda c: ring_step(1, 3, c))

    each_chunk(lambda c: fold_step(0, 0, c))
    each_chunk(lambda c: ring_last(1, c))

    def body(c):
        fold_step(0, 1, c)
        backward(c)

    each_chunk(body)
    each_chunk(lambda c: fold_step(0, 2, c))
    each_chunk(lambda c: fold_step(0, 3, c))

    each_chunk(lambda c: fold_step(1, 0, c))
    each_chunk(lambda c: fold_last(0, c))
    slot_step(0)

    def body(c):
        fold_step(1, 1, c)
        finish(0, c)

    each_chunk(body)
    slot_step(1)

    each_chunk(lambda c: fold_step(1, 2, c))
    slot_step(2)
    each_chunk(lambda c: fold_step(1, 3, c))
    slot_step(3)

    def body(c):
        for ab in (0, 1):
            pipe_copy(ab, c).wait_send()
            for j in range(1, experts):
                spread_copy(ab, c, j).wait_send()
            for t in range(HOPS):
                for d, sign in WAYS:
                    ring_copy(ab, t, c, d, sign).wait_send()
        for t in range(HOPS):
            for d, sign in WAYS:
                fold_copy(0, t, c, d, sign).wait_send()
        for j in range(1, experts):
            home_copy(0, c, j).wait_send()
        save_copy(0, c).wait()

    each_chunk(body)

    slot_last()
    fold_last(1, 0)

    def body(c):
        fold_last(1, c)
        finish(1, c - 1)

    lax.fori_loop(1, chunks, lambda c, carry: (body(c), carry)[1], 0)
    slot_finish()
    finish(1, chunks - 1)

    def body(c):
        for t in range(HOPS):
            for d, sign in WAYS:
                fold_copy(1, t, c, d, sign).wait_send()
        for j in range(1, experts):
            home_copy(1, c, j).wait_send()
        save_copy(1, c).wait()

    each_chunk(body)
    for d, sign in WAYS:
        for t in range(d, HOPS):
            slot_copy(d, t, sign).wait_send()
    for j in range(1, experts):
        last_copy(j).wait_send()


def on_device(
    section_acts,
    fwd_routes,
    fwd_gates,
    section_grads,
    bwd_routes,
    bwd_gates,
    saved_proj,
    w_gate,
    w_up,
    w_down,
):
    experts = lax.axis_size("expert") // GROUP
    _, tokens, model = section_acts.shape
    cap, hidden = saved_proj.shape[3], w_gate.shape[3]
    width = model // CHUNKS
    sources = saved_proj.shape[1]
    rows = (CHUNKS, experts, cap, width)
    lanes = 2 * experts * cap
    dma = pltpu.SemaphoreType.DMA
    hbm = pl.BlockSpec(memory_space=pl.ANY)
    vmem = pl.BlockSpec(memory_space=pltpu.VMEM)

    def as_row(array):
        return array.reshape(1, tokens)

    out_a, out_b, out_g = pl.pallas_call(
        kernel,
        out_shape=(
            jax.ShapeDtypeStruct(section_acts.shape, bf16),
            jax.ShapeDtypeStruct(section_grads.shape, bf16),
            jax.ShapeDtypeStruct((1, tokens), f32),
        ),
        in_specs=[hbm, hbm, vmem, vmem, vmem, vmem, hbm, hbm, hbm, hbm],
        out_specs=(hbm, hbm, vmem),
        scratch_shapes=[
            pltpu.VMEM((CHUNKS, tokens, width), bf16),
            pltpu.VMEM((CHUNKS, tokens, width), bf16),
            pltpu.VMEM(rows, bf16),
            pltpu.VMEM(rows, bf16),
            pltpu.VMEM((GROUP,) + rows, bf16),
            pltpu.VMEM((GROUP,) + rows, bf16),
            pltpu.VMEM((GROUP,) + rows, bf16),
            pltpu.VMEM((GROUP,) + rows, bf16),
            pltpu.VMEM((2, HOPS) + rows, bf16),
            pltpu.VMEM((2, HOPS) + rows, bf16),
            pltpu.VMEM(rows, bf16),
            pltpu.VMEM(rows, bf16),
            pltpu.VMEM((CHUNKS, tokens, width), bf16),
            pltpu.VMEM((CHUNKS, tokens, width), bf16),
            pltpu.VMEM((model, 2 * hidden), bf16),
            pltpu.VMEM((CHUNKS, hidden, width), bf16),
            pltpu.VMEM((sources, cap, 2 * hidden), bf16),
            pltpu.VMEM((PAIRS, 8, lanes), f32),
            pltpu.VMEM((2, HOPS, 8, lanes), f32),
            pltpu.VMEM((2, HOPS, 8, lanes), f32),
            pltpu.VMEM((8, lanes), f32),
            pltpu.VMEM((experts, 8, lanes), f32),
            dma((3 + CHUNKS,)),
            dma((2, CHUNKS)),
            dma((2, CHUNKS)),
            dma((2, CHUNKS)),
            dma((2, CHUNKS, experts - 1)),
            dma((2, CHUNKS, experts - 1)),
            dma((2, 2, HOPS * CHUNKS)),
            dma((2, 2, HOPS * CHUNKS)),
            dma((2, 2, HOPS * CHUNKS)),
            dma((2, 2, HOPS * CHUNKS)),
            dma((2, CHUNKS, experts - 1)),
            dma((2, CHUNKS, experts - 1)),
            dma((2, HOPS)),
            dma((2, HOPS)),
            dma((experts - 1,)),
            dma((experts - 1,)),
        ],
        compiler_params=pltpu.CompilerParams(
            collective_id=0, has_side_effects=True, vmem_limit_bytes=56 * 2**20
        ),
        cost_estimate=pl.CostEstimate(
            flops=2 * 2 * GROUP * experts * cap * model * 3 * hidden,
            bytes_accessed=2 * 3 * model * hidden + 8 * tokens * model,
            transcendentals=2 * GROUP * experts * cap * hidden,
        ),
        name="relay_experts",
    )(
        section_acts,
        section_grads,
        as_row(fwd_routes),
        as_row(fwd_gates),
        as_row(bwd_routes),
        as_row(bwd_gates),
        saved_proj,
        w_gate,
        w_up,
        w_down,
    )
    return out_a, out_b, out_g.reshape(1, tokens, 1)


def solution(mesh):
    tokens = P("pipe", "expert", None)
    weights = P("pipe", "expert", None, None)
    placed = (tokens,) * 6 + (P("pipe", None, "expert", None, None),) + (weights,) * 3
    return jax.shard_map(
        on_device, mesh=mesh, in_specs=placed, out_specs=(tokens,) * 3, check_vma=False
    )
```

time: 425 us -> 177 us (0.42)
  the two profiles are of different devices: /device:TPU:192 before, /device:TPU:24 now
where the time goes in v1:
time: 177 us
  Pallas kernels  173 us (98%)
  local copies, waits for them, and re-layouts  3.15 us (2%)
    pallas_call x1, Pallas kernels, on_device(): pl.pallas_call(kernel, out_shape=(jax.ShapeDtypeStruct(section_acts.shape...  173 us

profile of v1, /device:TPU:24, one launch (start us, length us, event | category | flops | bytes accessed | tf_op | source)
XLA Modules:
  0.0 177.1 jit_solution(8491818961424842170)
XLA Ops:
  0.6 173.3 %relay_experts.1 = (bf16[1,64,3584]{2,1,0:T(8,128)(2,1)}, bf16[1,64,3584]{2,1,0:T(8,128)(2,1)}, f32[1,64]{1,0:T(1,128)}) custom-call(bf16[1,64,3584]{2,1,0:T(8,128)(2,1)} %acts.1, bf16[1,64,3584]{2,1,0:T(8,128)(2,1)} %grads.1, s32[1,64]{1,0:T(1,128)} %bitcast.5, f32[1,64]{1,0:T(1,128)} %bitcast.6, s32[1,64]{1,0:T(1,128)} %bitcast.7, f32[1,64]{1,0:T(1,128)} %bitcast.8, ...), custom_call_target="tpu_custom_call" | custom-call | flops 2818572288 | bytes 4587520 | tf_op jit(solution)/shard_map/relay_experts/pallas_call | solution.py:567
  173.9 0.0 copy-start
  173.9 1.9 %copy.16 = bf16[1,64,3584]{2,1,0:T(8,128)(2,1)} copy(bf16[1,64,3584]{2,1,0:T(8,128)(2,1)} %get-tuple-element.12) | data formatting | bytes 917504
  175.8 0.0 copy-done
  175.8 0.0 copy-start.1
  175.8 0.8 copy.17
  176.5 0.0 copy-done.1
  176.6 0.5 copy.18
Async XLA Ops:
  173.9 1.9 %copy-start = (bf16[1,64,3584]{2,1,0:T(8,128)(2,1)S(1)}, bf16[1,64,3584]{2,1,0:T(8,128)(2,1)}, u32[]{:S(2)}) copy-start(bf16[1,64,3584]{2,1,0:T(8,128)(2,1)} %get-tuple-element.13) | copy-start | bytes 1376260
  175.8 0.8 copy-start.1

commit v2 on v1

v2 whole, which is shorter than its diff:
```python
import functools

import jax
import jax.numpy as jnp
from jax import lax
from jax.experimental import pallas as pl
from jax.experimental.pallas import tpu as pltpu
from jax.sharding import PartitionSpec as P

GROUP = 8
CHUNKS = 7
PAIRS = GROUP // 2
LANES = 128
HOPS = 4
MESH = pl.DeviceIdType.MESH
WAYS = ((0, 1), (1, -1))
f32 = jnp.float32
bf16 = jnp.bfloat16


def nt_dot(a, b):
    return lax.dot_general(a, b, (((1,), (1,)), ((), ())), preferred_element_type=f32)


def column_of(row):
    count = row.shape[1]
    shape = (count, count)
    eye = lax.broadcasted_iota(jnp.int32, shape, 0) == lax.broadcasted_iota(jnp.int32, shape, 1)
    return jnp.sum(jnp.where(eye, jnp.broadcast_to(row, shape), 0.0), axis=1, keepdims=True)


def row_of(column):
    count = column.shape[0]
    shape = (count, count)
    eye = lax.broadcasted_iota(jnp.int32, shape, 0) == lax.broadcasted_iota(jnp.int32, shape, 1)
    return jnp.sum(jnp.where(eye, jnp.broadcast_to(column, shape), 0.0), axis=0, keepdims=True)


def place_matrices(route_row, experts, cap):
    tokens = route_row.shape[1]
    slots = experts * cap
    routes = route_row.astype(f32)
    column = column_of(routes)
    at = lax.broadcasted_iota(jnp.int32, (tokens, tokens), 0)
    other = lax.broadcasted_iota(jnp.int32, (tokens, tokens), 1)
    slot = lax.broadcasted_iota(jnp.int32, (slots, tokens), 0)
    named = jnp.broadcast_to(routes, (slots, tokens)) == (slot // cap).astype(f32)
    before = jnp.dot(
        jnp.where(named, 1.0, 0.0).astype(bf16),
        jnp.where(at < other, 1.0, 0.0).astype(bf16),
        preferred_element_type=f32,
    )
    pack = jnp.where(named & (before == (slot % cap).astype(f32)), 1.0, 0.0).astype(bf16)
    slot = lax.broadcasted_iota(jnp.int32, (tokens, slots), 1)
    named = jnp.broadcast_to(column, (tokens, slots)) == (slot // cap).astype(f32)
    before = jnp.dot(
        jnp.where(other < at, 1.0, 0.0).astype(bf16),
        jnp.where(named, 1.0, 0.0).astype(bf16),
        preferred_element_type=f32,
    )
    unpack = jnp.where(named & (before == (slot % cap).astype(f32)), 1.0, 0.0).astype(bf16)
    return pack, unpack


def slices_of(model):
    tiles = model // LANES
    wide, slim = -(-tiles // GROUP) * LANES, tiles // GROUP * LANES
    many = tiles % GROUP
    starts = [min(r, many) * wide + max(r - many, 0) * slim for r in range(GROUP)]
    return [(start, wide if r < many else slim) for r, start in enumerate(starts)], many


def kernel(
    acts,
    grads,
    routes_a,
    gates_a,
    routes_b,
    gates_b,
    kept,
    w_gate,
    w_up,
    w_down,
    out_a,
    out_b,
    out_g,
    in_a,
    in_b,
    packed_a,
    packed_b,
    rows_a,
    local_b,
    cot_b,
    held,
    dhid_part,
    dhid_sums,
    hid_all,
    slice_part,
    slice_got,
    part_b,
    sums_b,
    back_a,
    back_b,
    whole_a,
    whole_b,
    both_w,
    saved,
    slot_own,
    slot_sent,
    slot_got,
    slot_fold,
    slot_back,
    load_sem,
    save_a_sem,
    save_b_sem,
    pipe_send,
    pipe_recv,
    spread_send,
    spread_recv,
    deal_send,
    deal_recv,
    cot_send,
    cot_recv,
    rows_send,
    rows_recv,
    dhid_send,
    dhid_recv,
    hid_send,
    hid_recv,
    slice_send,
    slice_recv,
    home_a_send,
    home_a_recv,
    fold_send,
    fold_recv,
    home_b_send,
    home_b_recv,
    slot_send,
    slot_recv,
    last_send,
    last_recv,
):
    stage = lax.axis_index("pipe")
    stages = lax.axis_size("pipe")
    index = lax.axis_index("expert")
    x = index // GROUP
    y = index % GROUP
    experts, chunks, cap, width = packed_a.shape
    model, hidden = both_w.shape[0], both_w.shape[1] // 2
    spread = experts * cap
    slices, many = slices_of(model)
    wide, slim = slices[0][1], slices[-1][1]
    shift = stage % 2 * many

    def slice_at(yy):
        return (yy + shift) % GROUP

    mine = slice_at(y)

    def with_slice(r, act):
        @pl.when(r < many)
        def _():
            act(pl.multiple_of(r * wide, LANES), wide)

        @pl.when(r >= many)
        def _():
            act(pl.multiple_of(many * wide + (r - many) * slim, LANES), slim)

    def column(xx):
        return {"expert": xx * GROUP + y}

    def ring(by):
        return {"expert": x * GROUP + (y + GROUP + by) % GROUP}

    def along(by):
        return {"pipe": (stage + stages + by) % stages}

    def remote(src, dst, send, recv, device):
        return pltpu.make_async_remote_copy(
            src_ref=src,
            dst_ref=dst,
            send_sem=send,
            recv_sem=recv,
            device_id=device,
            device_id_type=MESH,
        )

    def each(count, body, first=0):
        lax.fori_loop(first, count, lambda c, carry: (body(c), carry)[1], 0)

    def columns(c):
        return pl.ds(c * width if isinstance(c, int) else pl.multiple_of(c * width, LANES), width)

    barrier = pltpu.get_barrier_semaphore()
    partners = [along(1), along(-1)] + [ring(j) for j in range(1, GROUP)]
    partners += [column((x + j) % experts) for j in range(1, experts)]
    for partner in partners:
        pl.semaphore_signal(barrier, inc=1, device_id=partner, device_id_type=MESH)
    pl.semaphore_wait(barrier, len(partners))

    def pipe_copy(ab):
        source, target = ((acts, in_a), (grads, in_b))[ab]
        return remote(
            source.at[0], target, pipe_send.at[ab], pipe_recv.at[ab], along(1 - 2 * ab)
        )

    for ab in (1, 0):
        pipe_copy(ab).start()

    def deal_copy(j, start, size):
        return remote(
            w_down.at[0, 0, :, pl.ds(start, size)],
            held.at[y, :, pl.ds(0, size)],
            deal_send.at[j],
            deal_recv.at[j],
            ring(j),
        )

    def deal_own(start, size):
        return pltpu.make_async_copy(
            w_down.at[0, 0, :, pl.ds(start, size)], held.at[y, :, pl.ds(0, size)], deal_send.at[0]
        )

    def deal(j):
        with_slice(slice_at(y + j), lambda start, size: deal_copy(j, start, size).start())

    def deal_sent(j):
        with_slice(slice_at(y + j), lambda start, size: deal_copy(j, start, size).wait_send())

    def deal_got(start, size):
        def body(j):
            got = held.at[(y + GROUP - j) % GROUP, :, pl.ds(0, size)]
            remote(got, got, deal_send.at[j], deal_recv.at[j], ring(j)).wait_recv()

        deal_own(start, size).wait()
        each(GROUP, body, 1)

    each(GROUP, deal, 1)
    with_slice(mine, lambda start, size: deal_own(start, size).start())
    loads = [
        pltpu.make_async_copy(w_gate.at[0, 0], both_w.at[:, pl.ds(0, hidden)], load_sem.at[0]),
        pltpu.make_async_copy(w_up.at[0, 0], both_w.at[:, pl.ds(hidden, hidden)], load_sem.at[1]),
        pltpu.make_async_copy(kept.at[0, :, 0], saved, load_sem.at[2]),
    ]
    for load in loads:
        load.start()

    @pl.when(mine >= many)
    def _():
        held[:, :, slim:] = jnp.zeros((GROUP, hidden, wide - slim), bf16)
        cot_b[:, :, :, slim:] = jnp.zeros((GROUP, experts, cap, wide - slim), bf16)

    pack_a, unpack_a = place_matrices(routes_a[...], experts, cap)
    pack_b, unpack_b = place_matrices(routes_b[...], experts, cap)
    gate_a = column_of(gates_a[...])
    gate_b = column_of(gates_b[...].astype(bf16).astype(f32))

    def spread_copy(ab, j):
        to = (x + j) % experts
        return remote(
            (packed_a, packed_b)[ab].at[to],
            (rows_a.at[y, :, x], local_b.at[x])[ab],
            spread_send.at[ab, j - 1],
            spread_recv.at[ab, j - 1],
            column(to),
        )

    def spread_wait(ab):
        for j in range(1, experts):
            sender = (x + experts - j) % experts
            got = (rows_a.at[y, :, sender], local_b.at[sender])[ab]
            remote(
                got, got, spread_send.at[ab, j - 1], spread_recv.at[ab, j - 1], column(x)
            ).wait_recv()

    def packed_rows(pack, source, start, size):
        chosen = jnp.dot(pack, source[:, start : start + size], preferred_element_type=f32)
        return chosen.astype(bf16).reshape(experts, cap, size)

    pipe_copy(1).wait_recv()
    packed_b[:, many:, :, slim:] = jnp.zeros((experts, GROUP - many, cap, wide - slim), bf16)
    for r, (start, size) in enumerate(slices):
        packed_b[:, r, :, :size] = packed_rows(pack_b, in_b, start, size)
    for j in range(1, experts):
        spread_copy(1, j).start()
    local_b[x] = packed_b[x]
    pipe_copy(0).wait_recv()
    for c in range(chunks):
        packed_a[:, c] = packed_rows(pack_a, in_a, c * width, width)
    for j in range(1, experts):
        spread_copy(0, j).start()
    rows_a[y, :, x] = packed_a[x]

    def cot_copy(j, size):
        return remote(
            local_b.at[:, slice_at(y + j), :, pl.ds(0, size)],
            cot_b.at[y, :, :, pl.ds(0, size)],
            cot_send.at[j],
            cot_recv.at[j],
            ring(j),
        )

    def cot_own(size):
        return pltpu.make_async_copy(
            local_b.at[:, mine, :, pl.ds(0, size)],
            cot_b.at[y, :, :, pl.ds(0, size)],
            cot_send.at[0],
        )

    def cot_got(start, size):
        def body(j):
            got = cot_b.at[(y + GROUP - j) % GROUP, :, :, pl.ds(0, size)]
            remote(got, got, cot_send.at[j], cot_recv.at[j], ring(j)).wait_recv()

        cot_own(size).wait()
        each(GROUP, body, 1)

    def cot(j):
        with_slice(slice_at(y + j), lambda start, size: cot_copy(j, size).start())

    def cot_sent(j):
        with_slice(slice_at(y + j), lambda start, size: cot_copy(j, size).wait_send())

    def halves(ref, d, t, far):
        half = ref.shape[0] // 2
        return ref.at[pl.ds(d * half, half)] if t == far else ref

    class Gather:
        def __init__(self, blocks, send, recv):
            self.blocks, self.send, self.recv = blocks, send, recv
            self.count = blocks.shape[1]

        def copy(self, t, c, d, sign, on=0):
            at = self.blocks.at[(y + GROUP - sign * (t + on)) % GROUP, c]
            at = halves(at, d, t, HOPS - 1)
            k = t * self.count + c
            return remote(at, at, self.send.at[d, k], self.recv.at[d, k], ring(sign))

        def step(self, t, c):
            for d, sign in WAYS:
                if t:
                    self.copy(t - 1, c, d, sign, 1).wait_recv()
                self.copy(t, c, d, sign).start()

        def last(self, c):
            for d, sign in WAYS:
                self.copy(HOPS - 1, c, d, sign, 1).wait_recv()

        def sent(self, c):
            for t in range(HOPS):
                for d, sign in WAYS:
                    self.copy(t, c, d, sign).wait_send()

    class Fold:
        def __init__(self, part, sums, send, recv):
            self.part, self.sums, self.send, self.recv = part, sums, send, recv
            self.count = part.shape[1]

        def copy(self, t, c, d, sign):
            at = self.part.at[(y + GROUP + sign * (HOPS - t)) % GROUP, c]
            k = t * self.count + c
            return remote(
                halves(at, d, t, 0),
                halves(self.sums.at[d, t, c], d, t, 0),
                self.send.at[d, k],
                self.recv.at[d, k],
                ring(sign),
            )

        def step(self, t, c):
            half = self.part.shape[2] // 2
            for d, sign in WAYS:
                block = (y + GROUP + sign * (HOPS - t)) % GROUP
                if t:
                    self.copy(t - 1, c, d, sign).wait_recv()
                    at = pl.ds(d * half, half) if t == 1 else pl.ds(0, 2 * half)
                    self.part[block, c, at] = (
                        self.part[block, c, at].astype(f32)
                        + self.sums[d, t - 1, c, at].astype(f32)
                    ).astype(bf16)
                self.copy(t, c, d, sign).start()

        def total(self, c):
            for d, sign in WAYS:
                self.copy(HOPS - 1, c, d, sign).wait_recv()
            return (
                self.part[y, c].astype(f32)
                + self.sums[0, HOPS - 1, c].astype(f32)
                + self.sums[1, HOPS - 1, c].astype(f32)
            )

        def sent(self, c):
            for t in range(HOPS):
                for d, sign in WAYS:
                    self.copy(t, c, d, sign).wait_send()

    rows = Gather(rows_a, rows_send, rows_recv)
    hids = Gather(hid_all, hid_send, hid_recv)
    dhids = Fold(dhid_part, dhid_sums, dhid_send, dhid_recv)
    grads_x = Fold(part_b, sums_b, fold_send, fold_recv)

    def dhid_partial(p):
        here = cot_b[pl.ds(2 * p, 2)].reshape(2 * spread, wide)
        dhid = nt_dot(here, held[...].reshape(GROUP * hidden, wide)).astype(bf16)
        for g in range(GROUP):
            dhid_part[g, p] = dhid[:, g * hidden : (g + 1) * hidden].reshape(2, spread, hidden)

    def forward(p):
        pre = jnp.zeros((2 * spread, 2 * hidden), f32)
        for c in range(chunks):
            pre += jnp.dot(
                rows_a[pl.ds(2 * p, 2), c].reshape(2 * spread, width),
                both_w[pl.ds(c * width, width), :],
                preferred_element_type=f32,
            )
        pre_g, pre_u = pre[:, :hidden], pre[:, hidden:]
        hid = (pre_g * jax.nn.sigmoid(pre_g) * pre_u).astype(bf16)
        hid_all[y, p] = hid.reshape(2, spread, hidden)

    def forward_out(p):
        hid = jnp.concatenate(
            [hid_all[g, p].reshape(2 * spread, hidden) for g in range(GROUP)], axis=1
        )
        done = jnp.dot(
            hid, held[...].reshape(GROUP * hidden, wide), preferred_element_type=f32
        )
        slice_part[pl.ds(2 * p, 2)] = done.astype(bf16).reshape(2, experts, cap, wide)

    def backward(p):
        dhid = dhids.total(p).reshape(2 * spread, hidden)
        both = jnp.concatenate(
            [saved[j * GROUP + 2 * p + i] for i in (0, 1) for j in range(experts)], axis=0
        ).astype(f32)
        sg, su = both[:, :hidden], both[:, hidden:]
        sig = jax.nn.sigmoid(sg)
        act = sg * sig
        hid = (act * su).astype(bf16).astype(f32)
        slot_row = jnp.sum((hid * dhid).T, axis=0, keepdims=True)
        slot_own[p] = jnp.broadcast_to(slot_row, slot_own.shape[1:])
        d_g = (dhid * su * sig * (1.0 + sg * (1.0 - sig))).astype(bf16)
        d_u = (dhid * act).astype(bf16)
        d_both = jnp.concatenate([d_g, d_u], axis=1)
        for c in range(chunks):
            part_b[pl.ds(2 * p, 2), c] = (
                nt_dot(d_both, both_w[pl.ds(c * width, width), :])
                .astype(bf16)
                .reshape(2, experts, cap, width)
            )

    def slice_copy(j, size):
        return remote(
            slice_part.at[(y + j) % GROUP, :, :, pl.ds(0, size)],
            slice_got.at[mine, :, :, pl.ds(0, size)],
            slice_send.at[j],
            slice_recv.at[j],
            ring(j),
        )

    def home_a_copy(r, j):
        to = (x + j) % experts
        at = pl.ds(0, slices[r][1])
        return remote(
            slice_got.at[r, to, :, at],
            back_a.at[r, x, :, at],
            home_a_send.at[r, j - 1],
            home_a_recv.at[r, j - 1],
            column(to),
        )

    def home_a(r):
        off = (y + GROUP - (r + GROUP - shift) % GROUP) % GROUP

        @pl.when(off != 0)
        def _():
            got = slice_got.at[r, :, :, pl.ds(0, slices[r][1])]
            remote(got, got, slice_send.at[off], slice_recv.at[off], ring(1)).wait_recv()

        for j in range(1, experts):
            home_a_copy(r, j).start()
        back_a[r, x] = slice_got[r, x]

    def save_a(r):
        at = pl.ds(*slices[r])
        return pltpu.make_async_copy(whole_a.at[:, at], out_a.at[0, :, at], save_a_sem.at[r])

    def finish_a(r):
        start, size = slices[r]
        for j in range(1, experts):
            got = back_a.at[r, (x + experts - j) % experts, :, pl.ds(0, size)]
            remote(
                got, got, home_a_send.at[r, j - 1], home_a_recv.at[r, j - 1], column(x)
            ).wait_recv()
        picked = jnp.dot(
            unpack_a, back_a[r, :, :, :size].reshape(spread, size), preferred_element_type=f32
        )
        at = slice(start, start + size)
        whole_a[:, at] = (in_a[:, at].astype(f32) + gate_a * picked).astype(bf16)
        save_a(r).start()

    def home_b_copy(c, j):
        to = (x + j) % experts
        return remote(
            part_b.at[y, c, to],
            back_b.at[c, x],
            home_b_send.at[c, j - 1],
            home_b_recv.at[c, j - 1],
            column(to),
        )

    def home_b(c):
        part_b[y, c] = grads_x.total(c).astype(bf16)
        for j in range(1, experts):
            home_b_copy(c, j).start()
        back_b[c, x] = part_b[y, c, x]

    def save_b(c):
        return pltpu.make_async_copy(
            whole_b.at[:, columns(c)], out_b.at[0, :, columns(c)], save_b_sem.at[c]
        )

    def finish_b(c):
        for j in range(1, experts):
            got = back_b.at[c, (x + experts - j) % experts]
            remote(
                got, got, home_b_send.at[c, j - 1], home_b_recv.at[c, j - 1], column(x)
            ).wait_recv()
        picked = jnp.dot(unpack_b, back_b[c].reshape(spread, width), preferred_element_type=f32)
        whole_b[:, columns(c)] = (in_b[:, columns(c)].astype(f32) + gate_b * picked).astype(bf16)
        save_b(c).start()

    def slot_copy(d, t, sign):
        return remote(
            slot_sent.at[d, t],
            slot_got.at[d, t],
            slot_send.at[d, t],
            slot_recv.at[d, t],
            ring(sign),
        )

    def slot_step(t):
        for d, sign in WAYS:
            if t < d:
                continue
            pair = ((y + GROUP + sign * (HOPS - t)) % GROUP) // 2
            if t > d:
                slot_copy(d, t - 1, sign).wait_recv()
                slot_sent[d, t] = slot_own[pair] + slot_got[d, t - 1]
            else:
                slot_sent[d, t] = slot_own[pair]
            slot_copy(d, t, sign).start()

    def last_copy(j):
        return remote(
            slot_fold,
            slot_back.at[x],
            last_send.at[j - 1],
            last_recv.at[j - 1],
            column((x + j) % experts),
        )

    def slot_last():
        for d, sign in WAYS:
            slot_copy(d, HOPS - 1, sign).wait_recv()
        slot_fold[...] = slot_own[y // 2] + slot_got[0, HOPS - 1] + slot_got[1, HOPS - 1]
        for j in range(1, experts):
            last_copy(j).start()
        slot_back[x] = slot_fold[...]

    def slot_finish():
        for j in range(1, experts):
            got = slot_back.at[(x + experts - j) % experts]
            remote(
                got, got, last_send.at[j - 1], last_recv.at[j - 1], column(x)
            ).wait_recv()
        tokens = routes_b.shape[1]
        lanes = slot_back.shape[2]
        routes = column_of(routes_b[...].astype(f32))
        lane = lax.broadcasted_iota(jnp.int32, (tokens, spread), 1)
        taken = jnp.where(unpack_b > 0, (lane % cap).astype(f32), 0.0)
        slot = jnp.sum(taken, axis=1, keepdims=True)
        lane = lax.broadcasted_iota(jnp.int32, (tokens, lanes), 1)
        first = (y % 2) * spread + x * cap
        here = jnp.broadcast_to(slot, (tokens, lanes)) == (lane - first).astype(f32)
        total = jnp.zeros((tokens, lanes), f32)
        for e in range(experts):
            values = jnp.broadcast_to(slot_back[e][0:1], (tokens, lanes))
            total += jnp.where(here & (routes == float(e)), values, 0.0)
        out_g[...] = row_of(jnp.sum(total, axis=1, keepdims=True))

    spread_wait(1)
    each(GROUP, cot, 1)
    with_slice(mine, lambda start, size: cot_own(size).start())
    spread_wait(0)
    each(chunks, lambda c: rows.step(0, c))
    with_slice(mine, deal_got)
    with_slice(mine, cot_got)

    def body(c):
        rows.step(1, c)
        pl.when(c < PAIRS)(lambda: dhid_partial(c))

    each(chunks, body)

    def body(c):
        rows.step(2, c)
        pl.when(c < PAIRS)(lambda: dhids.step(0, c))

    each(chunks, body)

    def body(c):
        rows.step(3, c)
        pl.when(c < PAIRS)(lambda: dhids.step(1, c))

    each(chunks, body)
    each(PAIRS, lambda c: dhids.step(2, c))
    each(chunks, rows.last)
    for load in loads:
        load.wait()

    def body(p):
        forward(p)
        hids.step(0, p)
        dhids.step(3, p)

    each(PAIRS, body)

    def far_first(k):
        return (y // 2 + PAIRS // 2 + k) % PAIRS

    backward(far_first(0))
    each(chunks, lambda c: grads_x.step(0, c))
    each(PAIRS, lambda c: hids.step(1, c))

    def body(k):
        backward(far_first(k))

        @pl.when(k == 1)
        def _():
            each(PAIRS, lambda c: hids.step(2, c))

        @pl.when(k == 2)
        def _():
            each(PAIRS, lambda c: hids.step(3, c))

    each(PAIRS, body, 1)
    slot_step(0)
    each(chunks, lambda c: grads_x.step(1, c))
    slot_step(1)

    each(PAIRS, hids.last)
    each(PAIRS, forward_out)

    def body(start, size):
        each(GROUP, lambda j: slice_copy(j, size).start(), 1)

    with_slice(mine, body)
    slice_got[mine] = slice_part[y]
    each(chunks, lambda c: grads_x.step(2, c))
    slot_step(2)
    for r in range(GROUP):
        home_a(r)
    for r in range(GROUP):
        finish_a(r)
    each(chunks, lambda c: grads_x.step(3, c))
    slot_step(3)

    for ab in (0, 1):
        pipe_copy(ab).wait_send()
        for j in range(1, experts):
            spread_copy(ab, j).wait_send()
    each(GROUP, deal_sent, 1)
    each(GROUP, cot_sent, 1)
    each(chunks, rows.sent)
    each(PAIRS, dhids.sent)
    each(PAIRS, hids.sent)

    def body(start, size):
        each(GROUP, lambda j: slice_copy(j, size).wait_send(), 1)

    with_slice(mine, body)
    for r in range(GROUP):
        for j in range(1, experts):
            home_a_copy(r, j).wait_send()
        save_a(r).wait()

    slot_last()
    home_b(0)

    def body(c):
        home_b(c)
        finish_b(c - 1)

    each(chunks, body, 1)
    slot_finish()
    finish_b(chunks - 1)

    def body(c):
        grads_x.sent(c)
        for j in range(1, experts):
            home_b_copy(c, j).wait_send()
        save_b(c).wait()

    each(chunks, body)
    for d, sign in WAYS:
        for t in range(d, HOPS):
            slot_copy(d, t, sign).wait_send()
    for j in range(1, experts):
        last_copy(j).wait_send()


def on_device(
    section_acts,
    fwd_routes,
    fwd_gates,
    section_grads,
    bwd_routes,
    bwd_gates,
    saved_proj,
    w_gate,
    w_up,
    w_down,
):
    experts = lax.axis_size("expert") // GROUP
    _, tokens, model = section_acts.shape
    cap, hidden = saved_proj.shape[3], w_gate.shape[3]
    width = model // CHUNKS
    sources = saved_proj.shape[1]
    spread = experts * cap
    lanes = 2 * spread
    wide = slices_of(model)[0][0][1]
    whole = (tokens, model)
    by_slice = (experts, GROUP, cap, wide)
    by_chunk = (experts, CHUNKS, cap, width)
    blocks = (CHUNKS, experts, cap, width)
    hids = (PAIRS, 2, spread, hidden)
    dma = pltpu.SemaphoreType.DMA
    hbm = pl.BlockSpec(memory_space=pl.ANY)
    vmem = pl.BlockSpec(memory_space=pltpu.VMEM)

    def as_row(array):
        return array.reshape(1, tokens)

    def two(*shape):
        return [dma(shape), dma(shape)]

    shapes = [
        whole,
        whole,
        by_chunk,
        by_slice,
        (GROUP,) + blocks,
        by_slice,
        (GROUP, experts, cap, wide),
        (GROUP, hidden, wide),
        (GROUP,) + hids,
        (2, HOPS) + hids,
        (GROUP,) + hids,
        (GROUP, experts, cap, wide),
        (GROUP, experts, cap, wide),
        (GROUP,) + blocks,
        (2, HOPS) + blocks,
        (GROUP, experts, cap, wide),
        blocks,
        whole,
        whole,
        (model, 2 * hidden),
        (sources, cap, 2 * hidden),
    ]
    slots = [(PAIRS, 8, lanes), (2, HOPS, 8, lanes), (2, HOPS, 8, lanes), (8, lanes)]
    slots.append((experts, 8, lanes))

    out_a, out_b, out_g = pl.pallas_call(
        kernel,
        out_shape=(
            jax.ShapeDtypeStruct(section_acts.shape, bf16),
            jax.ShapeDtypeStruct(section_grads.shape, bf16),
            jax.ShapeDtypeStruct((1, tokens), f32),
        ),
        in_specs=[hbm, hbm, vmem, vmem, vmem, vmem, hbm, hbm, hbm, hbm],
        out_specs=(hbm, hbm, vmem),
        scratch_shapes=[pltpu.VMEM(shape, bf16) for shape in shapes]
        + [pltpu.VMEM(shape, f32) for shape in slots]
        + [dma((3,)), dma((GROUP,)), dma((CHUNKS,))]
        + two(2)
        + two(2, experts - 1)
        + two(GROUP)
        + two(GROUP)
        + two(2, HOPS * CHUNKS)
        + two(2, HOPS * PAIRS)
        + two(2, HOPS * PAIRS)
        + two(GROUP)
        + two(GROUP, experts - 1)
        + two(2, HOPS * CHUNKS)
        + two(CHUNKS, experts - 1)
        + two(2, HOPS)
        + two(experts - 1),
        compiler_params=pltpu.CompilerParams(
            collective_id=0, has_side_effects=True, vmem_limit_bytes=56 * 2**20
        ),
        cost_estimate=pl.CostEstimate(
            flops=2 * 2 * GROUP * spread * model * 3 * hidden,
            bytes_accessed=2 * 3 * model * hidden + 8 * tokens * model,
            transcendentals=2 * GROUP * spread * hidden,
        ),
        name="relay_experts",
    )(
        section_acts,
        section_grads,
        as_row(fwd_routes),
        as_row(fwd_gates),
        as_row(bwd_routes),
        as_row(bwd_gates),
        saved_proj,
        w_gate,
        w_up,
        w_down,
    )
    return out_a, out_b, out_g.reshape(1, tokens, 1)


def solution(mesh):
    tokens = P("pipe", "expert", None)
    weights = P("pipe", "expert", None, None)
    placed = (tokens,) * 6 + (P("pipe", None, "expert", None, None),) + (weights,) * 3
    return jax.shard_map(
        on_device, mesh=mesh, in_specs=placed, out_specs=(tokens,) * 3, check_vma=False
    )
```

time: 177 us -> 168 us (0.949)
  the two profiles are of different devices: /device:TPU:24 before, /device:TPU:128 now
where the time goes in v2:
time: 168 us
  Pallas kernels  165 us (98%)
  local copies, waits for them, and re-layouts  3.15 us (2%)
    pallas_call x1, Pallas kernels, on_device(): pl.pallas_call(kernel, out_shape=(jax.ShapeDtypeStruct(section_acts.shape...  165 us

profile of v2, /device:TPU:128, one launch (start us, length us, event | category | flops | bytes accessed | tf_op | source)
XLA Modules:
  0.0 168.3 jit_solution(5146855024748131197)
XLA Ops:
  0.6 164.5 %relay_experts.1 = (bf16[1,64,3584]{2,1,0:T(8,128)(2,1)}, bf16[1,64,3584]{2,1,0:T(8,128)(2,1)}, f32[1,64]{1,0:T(1,128)}) custom-call(bf16[1,64,3584]{2,1,0:T(8,128)(2,1)} %acts.1, bf16[1,64,3584]{2,1,0:T(8,128)(2,1)} %grads.1, s32[1,64]{1,0:T(1,128)} %bitcast.5, f32[1,64]{1,0:T(1,128)} %bitcast.6, s32[1,64]{1,0:T(1,128)} %bitcast.7, f32[1,64]{1,0:T(1,128)} %bitcast.8, ...), custom_call_target="tpu_custom_call" | custom-call | flops 2818572288 | bytes 4587520 | tf_op jit(solution)/shard_map/relay_experts/pallas_call | solution.py:772
  165.2 0.0 copy-start
  165.2 1.9 %copy.16 = bf16[1,64,3584]{2,1,0:T(8,128)(2,1)} copy(bf16[1,64,3584]{2,1,0:T(8,128)(2,1)} %get-tuple-element.12) | data formatting | bytes 917504
  167.0 0.0 copy-done
  167.0 0.0 copy-start.1
  167.0 0.8 copy.17
  167.8 0.0 copy-done.1
  167.8 0.5 copy.18
Async XLA Ops:
  165.2 1.9 %copy-start = (bf16[1,64,3584]{2,1,0:T(8,128)(2,1)S(1)}, bf16[1,64,3584]{2,1,0:T(8,128)(2,1)}, u32[]{:S(2)}) copy-start(bf16[1,64,3584]{2,1,0:T(8,128)(2,1)} %get-tuple-element.13) | copy-start | bytes 1376260
  167.0 0.8 copy-start.1

commit v3 on v2

--- a/solution.py
+++ b/solution.py
@@ -100,7 +100,7 @@
     part_b,
     sums_b,
     back_a,
-    back_b,
+    straight,
     whole_a,
     whole_b,
     both_w,
@@ -133,8 +133,8 @@
     home_a_recv,
     fold_send,
     fold_recv,
-    home_b_send,
-    home_b_recv,
+    straight_send,
+    straight_recv,
     slot_send,
     slot_recv,
     last_send,
@@ -169,6 +169,9 @@
     def column(xx):
         return {"expert": xx * GROUP + y}
 
+    def beside(j, by):
+        return {"expert": (x + j) % experts * GROUP + (y + GROUP + by) % GROUP}
+
     def ring(by):
         return {"expert": x * GROUP + (y + GROUP + by) % GROUP}
 
@@ -194,6 +197,7 @@
     barrier = pltpu.get_barrier_semaphore()
     partners = [along(1), along(-1)] + [ring(j) for j in range(1, GROUP)]
     partners += [column((x + j) % experts) for j in range(1, experts)]
+    partners += [beside(j, sign) for j in range(1, experts) for _, sign in WAYS]
     for partner in partners:
         pl.semaphore_signal(barrier, inc=1, device_id=partner, device_id_type=MESH)
     pl.semaphore_wait(barrier, len(partners))
@@ -204,7 +208,7 @@
             source.at[0], target, pipe_send.at[ab], pipe_recv.at[ab], along(1 - 2 * ab)
         )
 
-    for ab in (1, 0):
+    for ab in (0, 1):
         pipe_copy(ab).start()
 
     def deal_copy(j, start, size):
@@ -277,6 +281,12 @@
         chosen = jnp.dot(pack, source[:, start : start + size], preferred_element_type=f32)
         return chosen.astype(bf16).reshape(experts, cap, size)
 
+    pipe_copy(0).wait_recv()
+    for c in range(chunks):
+        packed_a[:, c] = packed_rows(pack_a, in_a, c * width, width)
+    for j in range(1, experts):
+        spread_copy(0, j).start()
+    rows_a[y, :, x] = packed_a[x]
     pipe_copy(1).wait_recv()
     packed_b[:, many:, :, slim:] = jnp.zeros((experts, GROUP - many, cap, wide - slim), bf16)
     for r, (start, size) in enumerate(slices):
@@ -284,12 +294,6 @@
     for j in range(1, experts):
         spread_copy(1, j).start()
     local_b[x] = packed_b[x]
-    pipe_copy(0).wait_recv()
-    for c in range(chunks):
-        packed_a[:, c] = packed_rows(pack_a, in_a, c * width, width)
-    for j in range(1, experts):
-        spread_copy(0, j).start()
-    rows_a[y, :, x] = packed_a[x]
 
     def cot_copy(j, size):
         return remote(
@@ -367,7 +371,7 @@
                 ring(sign),
             )
 
-        def step(self, t, c):
+        def step(self, t, c, straight=None):
             half = self.part.shape[2] // 2
             for d, sign in WAYS:
                 block = (y + GROUP + sign * (HOPS - t)) % GROUP
@@ -378,7 +382,10 @@
                         self.part[block, c, at].astype(f32)
                         + self.sums[d, t - 1, c, at].astype(f32)
                     ).astype(bf16)
-                self.copy(t, c, d, sign).start()
+                if straight is None:
+                    self.copy(t, c, d, sign).start()
+                else:
+                    straight(c, d, sign, block)
 
         def total(self, c):
             for d, sign in WAYS:
@@ -389,8 +396,8 @@
                 + self.sums[1, HOPS - 1, c].astype(f32)
             )
 
-        def sent(self, c):
-            for t in range(HOPS):
+        def sent(self, c, hops=HOPS):
+            for t in range(hops):
                 for d, sign in WAYS:
                     self.copy(t, c, d, sign).wait_send()
 
@@ -497,34 +504,51 @@
         whole_a[:, at] = (in_a[:, at].astype(f32) + gate_a * picked).astype(bf16)
         save_a(r).start()
 
-    def home_b_copy(c, j):
-        to = (x + j) % experts
-        return remote(
-            part_b.at[y, c, to],
-            back_b.at[c, x],
-            home_b_send.at[c, j - 1],
-            home_b_recv.at[c, j - 1],
-            column(to),
-        )
-
-    def home_b(c):
-        part_b[y, c] = grads_x.total(c).astype(bf16)
-        for j in range(1, experts):
-            home_b_copy(c, j).start()
-        back_b[c, x] = part_b[y, c, x]
-
     def save_b(c):
         return pltpu.make_async_copy(
             whole_b.at[:, columns(c)], out_b.at[0, :, columns(c)], save_b_sem.at[c]
         )
 
-    def finish_b(c):
+    def straight_copy(c, d, j, sign, block):
+        return remote(
+            part_b.at[block, c, (x + j) % experts],
+            straight.at[c, d, x],
+            straight_send.at[c, d, j],
+            straight_recv.at[c],
+            beside(j, sign),
+        )
+
+    def straight_own(c):
+        return pltpu.make_async_copy(
+            part_b.at[y, c, x], straight.at[c, 2, x], straight_recv.at[c]
+        )
+
+    def straight_mine(c):
+        straight_own(c).start()
         for j in range(1, experts):
-            got = back_b.at[c, (x + experts - j) % experts]
-            remote(
-                got, got, home_b_send.at[c, j - 1], home_b_recv.at[c, j - 1], column(x)
-            ).wait_recv()
-        picked = jnp.dot(unpack_b, back_b[c].reshape(spread, width), preferred_element_type=f32)
+            straight_copy(c, 2, j, 0, y).start()
+
+    def straight_last(c, d, sign, block):
+        for j in range(experts):
+            straight_copy(c, d, j, sign, block).start()
+
+    def straight_sent(c):
+        for d, sign in WAYS:
+            block = (y + GROUP + sign) % GROUP
+            for j in range(experts):
+                straight_copy(c, d, j, sign, block).wait_send()
+        for j in range(1, experts):
+            straight_copy(c, 2, j, 0, y).wait_send()
+
+    def straight_finish(c):
+        got = straight.at[c]
+        remote(
+            got, got, straight_send.at[c, 0, 0], straight_recv.at[c], column(x)
+        ).wait_recv()
+        picked = jnp.zeros((spread, width), f32)
+        for d in range(3):
+            rows_d = straight[c, d].reshape(spread, width)
+            picked += jnp.dot(unpack_b, rows_d, preferred_element_type=f32)
         whole_b[:, columns(c)] = (in_b[:, columns(c)].astype(f32) + gate_b * picked).astype(bf16)
         save_b(c).start()
 
@@ -587,81 +611,69 @@
             total += jnp.where(here & (routes == float(e)), values, 0.0)
         out_g[...] = row_of(jnp.sum(total, axis=1, keepdims=True))
 
+    spread_wait(0)
+    for t in range(HOPS):
+        each(chunks, functools.partial(rows.step, t))
     spread_wait(1)
     each(GROUP, cot, 1)
     with_slice(mine, lambda start, size: cot_own(size).start())
-    spread_wait(0)
-    each(chunks, lambda c: rows.step(0, c))
-    with_slice(mine, deal_got)
-    with_slice(mine, cot_got)
-
-    def body(c):
-        rows.step(1, c)
-        pl.when(c < PAIRS)(lambda: dhid_partial(c))
-
-    each(chunks, body)
-
-    def body(c):
-        rows.step(2, c)
-        pl.when(c < PAIRS)(lambda: dhids.step(0, c))
-
-    each(chunks, body)
-
-    def body(c):
-        rows.step(3, c)
-        pl.when(c < PAIRS)(lambda: dhids.step(1, c))
-
-    each(chunks, body)
-    each(PAIRS, lambda c: dhids.step(2, c))
-    each(chunks, rows.last)
     for load in loads:
         load.wait()
+    each(chunks, rows.last)
 
     def body(p):
         forward(p)
         hids.step(0, p)
-        dhids.step(3, p)
 
     each(PAIRS, body)
-
-    def far_first(k):
-        return (y // 2 + PAIRS // 2 + k) % PAIRS
-
-    backward(far_first(0))
+    with_slice(mine, deal_got)
+    with_slice(mine, cot_got)
+
+    def body(p):
+        dhid_partial(p)
+        dhids.step(0, p)
+        hids.step(1, p)
+
+    each(PAIRS, body)
+
+    def body(p):
+        hids.step(2, p)
+        dhids.step(1, p)
+
+    each(PAIRS, body)
+
+    def body(p):
+        hids.step(3, p)
+        dhids.step(2, p)
+
+    each(PAIRS, body)
+    each(PAIRS, lambda p: dhids.step(3, p))
+
+    each(PAIRS, hids.last)
+    each(PAIRS, forward_out)
+
+    def body(start, size):
+        each(GROUP, lambda j: slice_copy(j, size).start(), 1)
+
+    with_slice(mine, body)
+    slice_got[mine] = slice_part[y]
+
+    backward((y // 2 + PAIRS // 2) % PAIRS)
     each(chunks, lambda c: grads_x.step(0, c))
-    each(PAIRS, lambda c: hids.step(1, c))
-
-    def body(k):
-        backward(far_first(k))
-
-        @pl.when(k == 1)
-        def _():
-            each(PAIRS, lambda c: hids.step(2, c))
-
-        @pl.when(k == 2)
-        def _():
-            each(PAIRS, lambda c: hids.step(3, c))
-
-    each(PAIRS, body, 1)
+    backward((y // 2 + PAIRS // 2 + 3 - 2 * (y % 2)) % PAIRS)
+    backward((y // 2 + PAIRS // 2 + 1 + 2 * (y % 2)) % PAIRS)
+    backward(y // 2)
     slot_step(0)
     each(chunks, lambda c: grads_x.step(1, c))
     slot_step(1)
-
-    each(PAIRS, hids.last)
-    each(PAIRS, forward_out)
-
-    def body(start, size):
-        each(GROUP, lambda j: slice_copy(j, size).start(), 1)
-
-    with_slice(mine, body)
-    slice_got[mine] = slice_part[y]
+    each(chunks, straight_mine)
+    for r in range(GROUP):
+        home_a(r)
     each(chunks, lambda c: grads_x.step(2, c))
     slot_step(2)
     for r in range(GROUP):
-        home_a(r)
-    for r in range(GROUP):
         finish_a(r)
-    each(chunks, lambda c: grads_x.step(3, c))
+    each(chunks, lambda c: grads_x.step(3, c, straight_last))
     slot_step(3)
 
     for ab in (0, 1):
@@ -678,27 +690,19 @@
         each(GROUP, lambda j: slice_copy(j, size).wait_send(), 1)
 
     with_slice(mine, body)
+
+    slot_last()
+
     for r in range(GROUP):
         for j in range(1, experts):
             home_a_copy(r, j).wait_send()
         save_a(r).wait()
-
-    slot_last()
-    home_b(0)
+    each(chunks, lambda c: grads_x.sent(c, HOPS - 1))
+    slot_finish()
 
     def body(c):
-        home_b(c)
-        finish_b(c - 1)
-
-    each(chunks, body, 1)
-    slot_finish()
-    finish_b(chunks - 1)
-
-    def body(c):
-        grads_x.sent(c)
-        for j in range(1, experts):
-            home_b_copy(c, j).wait_send()
-        save_b(c).wait()
+        straight_finish(c)
+        straight_sent(c)
 
     each(chunks, body)
     for d, sign in WAYS:
@@ -706,6 +710,7 @@
             slot_copy(d, t, sign).wait_send()
     for j in range(1, experts):
         last_copy(j).wait_send()
+    each(chunks, lambda c: save_b(c).wait())
 
 
 def on_device(
@@ -760,7 +765,7 @@
         (GROUP,) + blocks,
         (2, HOPS) + blocks,
         (GROUP, experts, cap, wide),
-        blocks,
+        (CHUNKS, 3, experts, cap, width),
         whole,
         whole,
         (model, 2 * hidden),
@@ -791,7 +796,7 @@
         + two(GROUP)
         + two(GROUP, experts - 1)
         + two(2, HOPS * CHUNKS)
-        + two(CHUNKS, experts - 1)
+        + [dma((CHUNKS, 3, experts)), dma((CHUNKS,))]
         + two(2, HOPS)
         + two(experts - 1),
         compiler_params=pltpu.CompilerParams(

time: 168 us -> 156 us (0.929)
  the two profiles are of different devices: /device:TPU:128 before, /device:TPU:192 now
where the time goes in v3:
time: 156 us
  Pallas kernels  152 us (97%)
  local copies, waits for them, and re-layouts  3.15 us (2%)
    pallas_call x1, Pallas kernels, on_device(): pl.pallas_call(kernel, out_shape=(jax.ShapeDtypeStruct(section_acts.shape...  152 us
    unnamed x7, local copies, waits for them, and re-layouts  3.15 us

profile of v3, /device:TPU:192, one launch (start us, length us, event | category | flops | bytes accessed | tf_op | source)
XLA Modules:
  0.0 156.1 jit_solution(1563053931384469655)
XLA Ops:
  0.6 152.3 %relay_experts.1 = (bf16[1,64,3584]{2,1,0:T(8,128)(2,1)}, bf16[1,64,3584]{2,1,0:T(8,128)(2,1)}, f32[1,64]{1,0:T(1,128)}) custom-call(bf16[1,64,3584]{2,1,0:T(8,128)(2,1)} %acts.1, bf16[1,64,3584]{2,1,0:T(8,128)(2,1)} %grads.1, s32[1,64]{1,0:T(1,128)} %bitcast.5, f32[1,64]{1,0:T(1,128)} %bitcast.6, s32[1,64]{1,0:T(1,128)} %bitcast.7, f32[1,64]{1,0:T(1,128)} %bitcast.8, ...), custom_call_target="tpu_custom_call" | custom-call | flops 2818572288 | bytes 4587520 | tf_op jit(solution)/shard_map/relay_experts/pallas_call | solution.py:777
  152.9 0.0 copy-start
  152.9 1.9 %copy.16 = bf16[1,64,3584]{2,1,0:T(8,128)(2,1)} copy(bf16[1,64,3584]{2,1,0:T(8,128)(2,1)} %get-tuple-element.12) | data formatting | bytes 917504
  154.8 0.0 copy-done
  154.8 0.0 copy-start.1
  154.8 0.8 copy.17
  155.6 0.0 copy-done.1
  155.6 0.5 copy.18
Async XLA Ops:
  152.9 1.9 %copy-start = (bf16[1,64,3584]{2,1,0:T(8,128)(2,1)S(1)}, bf16[1,64,3584]{2,1,0:T(8,128)(2,1)}, u32[]{:S(2)}) copy-start(bf16[1,64,3584]{2,1,0:T(8,128)(2,1)} %get-tuple-element.13) | copy-start | bytes 1376260
  154.8 0.8 copy-start.1

commit v4 on v3

--- a/solution.py
+++ b/solution.py
@@ -8,7 +8,7 @@
 from jax.sharding import PartitionSpec as P
 
 GROUP = 8
-CHUNKS = 7
+CHUNKS = 4
 PAIRS = GROUP // 2
 LANES = 128
 HOPS = 4
@@ -647,15 +647,18 @@
         dhids.step(2, p)
 
     each(PAIRS, body)
-    each(PAIRS, lambda p: dhids.step(3, p))
-
-    each(PAIRS, hids.last)
-    each(PAIRS, forward_out)
-
-    def body(start, size):
-        each(GROUP, lambda j: slice_copy(j, size).start(), 1)
-
-    with_slice(mine, body)
+
+    def body(p):
+        dhids.step(3, p)
+        hids.last(p)
+        forward_out(p)
+        for i in (0, 1):
+            j = (2 * p + i + GROUP - y) % GROUP
+            pl.when(j != 0)(
+                lambda: with_slice(mine, lambda start, size: slice_copy(j, size).start())
+            )
+
+    each(PAIRS, body)
     slice_got[mine] = slice_part[y]
 
     backward((y // 2 + PAIRS // 2) % PAIRS)
@@ -664,17 +667,17 @@
     backward((y // 2 + PAIRS // 2 + 1 + 2 * (y % 2)) % PAIRS)
     backward(y // 2)
     slot_step(0)
+    each(chunks, straight_mine)
     each(chunks, lambda c: grads_x.step(1, c))
     slot_step(1)
-    each(chunks, straight_mine)
     for r in range(GROUP):
         home_a(r)
     each(chunks, lambda c: grads_x.step(2, c))
     slot_step(2)
+    each(chunks, lambda c: grads_x.step(3, c, straight_last))
+    slot_step(3)
     for r in range(GROUP):
         finish_a(r)
-    each(chunks, lambda c: grads_x.step(3, c, straight_last))
-    slot_step(3)
 
     for ab in (0, 1):
         pipe_copy(ab).wait_send()

time: 156 us -> 155 us (level)
  the two profiles are of different devices: /device:TPU:192 before, /device:TPU:264 now
where the time goes in v4:
time: 155 us; the launch traced here: 154 us
  Pallas kernels  151 us (97%)
  local copies, waits for them, and re-layouts  3.15 us (2%)
    pallas_call x1, Pallas kernels, on_device(): pl.pallas_call(kernel, out_shape=(jax.ShapeDtypeStruct(section_acts.shape...  151 us
    unnamed x7, local copies, waits for them, and re-layouts  3.15 us

profile of v4, /device:TPU:264, one launch (start us, length us, event | category | flops | bytes accessed | tf_op | source)
XLA Modules:
  0.0 154.4 jit_solution(16599551430299846882)
XLA Ops:
  0.6 150.6 %relay_experts.1 = (bf16[1,64,3584]{2,1,0:T(8,128)(2,1)}, bf16[1,64,3584]{2,1,0:T(8,128)(2,1)}, f32[1,64]{1,0:T(1,128)}) custom-call(bf16[1,64,3584]{2,1,0:T(8,128)(2,1)} %acts.1, bf16[1,64,3584]{2,1,0:T(8,128)(2,1)} %grads.1, s32[1,64]{1,0:T(1,128)} %bitcast.5, f32[1,64]{1,0:T(1,128)} %bitcast.6, s32[1,64]{1,0:T(1,128)} %bitcast.7, f32[1,64]{1,0:T(1,128)} %bitcast.8, ...), custom_call_target="tpu_custom_call" | custom-call | flops 2818572288 | bytes 4587520 | tf_op jit(solution)/shard_map/relay_experts/pallas_call | solution.py:780
  151.3 0.0 copy-start
  151.3 1.9 %copy.16 = bf16[1,64,3584]{2,1,0:T(8,128)(2,1)} copy(bf16[1,64,3584]{2,1,0:T(8,128)(2,1)} %get-tuple-element.12) | data formatting | bytes 917504
  153.1 0.0 copy-done
  153.1 0.0 copy-start.1
  153.1 0.8 copy.17
  153.9 0.0 copy-done.1
  153.9 0.5 copy.18
Async XLA Ops:
  151.3 1.9 %copy-start = (bf16[1,64,3584]{2,1,0:T(8,128)(2,1)S(1)}, bf16[1,64,3584]{2,1,0:T(8,128)(2,1)}, u32[]{:S(2)}) copy-start(bf16[1,64,3584]{2,1,0:T(8,128)(2,1)} %get-tuple-element.13) | copy-start | bytes 1376260
  153.1 0.8 copy-start.1

commit v5 on v4

--- a/solution.py
+++ b/solution.py
@@ -101,8 +101,6 @@
     sums_b,
     back_a,
     straight,
-    whole_a,
-    whole_b,
     both_w,
     saved,
     slot_own,
@@ -111,8 +109,6 @@
     slot_fold,
     slot_back,
     load_sem,
-    save_a_sem,
-    save_b_sem,
     pipe_send,
     pipe_recv,
     spread_send,
@@ -486,10 +482,6 @@
             home_a_copy(r, j).start()
         back_a[r, x] = slice_got[r, x]
 
-    def save_a(r):
-        at = pl.ds(*slices[r])
-        return pltpu.make_async_copy(whole_a.at[:, at], out_a.at[0, :, at], save_a_sem.at[r])
-
     def finish_a(r):
         start, size = slices[r]
         for j in range(1, experts):
@@ -501,13 +493,7 @@
             unpack_a, back_a[r, :, :, :size].reshape(spread, size), preferred_element_type=f32
         )
         at = slice(start, start + size)
-        whole_a[:, at] = (in_a[:, at].astype(f32) + gate_a * picked).astype(bf16)
-        save_a(r).start()
-
-    def save_b(c):
-        return pltpu.make_async_copy(
-            whole_b.at[:, columns(c)], out_b.at[0, :, columns(c)], save_b_sem.at[c]
-        )
+        out_a[0, :, at] = (in_a[:, at].astype(f32) + gate_a * picked).astype(bf16)
 
     def straight_copy(c, d, j, sign, block):
         return remote(
@@ -549,8 +535,7 @@
         for d in range(3):
             rows_d = straight[c, d].reshape(spread, width)
             picked += jnp.dot(unpack_b, rows_d, preferred_element_type=f32)
-        whole_b[:, columns(c)] = (in_b[:, columns(c)].astype(f32) + gate_b * picked).astype(bf16)
-        save_b(c).start()
+        out_b[0, :, columns(c)] = (in_b[:, columns(c)].astype(f32) + gate_b * picked).astype(bf16)
 
     def slot_copy(d, t, sign):
         return remote(
@@ -699,7 +684,6 @@
     for r in range(GROUP):
         for j in range(1, experts):
             home_a_copy(r, j).wait_send()
-        save_a(r).wait()
     each(chunks, lambda c: grads_x.sent(c, HOPS - 1))
     slot_finish()
 
@@ -713,7 +697,6 @@
             slot_copy(d, t, sign).wait_send()
     for j in range(1, experts):
         last_copy(j).wait_send()
-    each(chunks, lambda c: save_b(c).wait())
 
 
 def on_device(
@@ -742,7 +725,7 @@
     blocks = (CHUNKS, experts, cap, width)
     hids = (PAIRS, 2, spread, hidden)
     dma = pltpu.SemaphoreType.DMA
-    hbm = pl.BlockSpec(memory_space=pl.ANY)
+    hbm = pl.BlockSpec(memory_space=pltpu.HBM)
     vmem = pl.BlockSpec(memory_space=pltpu.VMEM)
 
     def as_row(array):
@@ -769,8 +752,6 @@
         (2, HOPS) + blocks,
         (GROUP, experts, cap, wide),
         (CHUNKS, 3, experts, cap, width),
-        whole,
-        whole,
         (model, 2 * hidden),
         (sources, cap, 2 * hidden),
     ]
@@ -780,15 +761,15 @@
     out_a, out_b, out_g = pl.pallas_call(
         kernel,
         out_shape=(
-            jax.ShapeDtypeStruct(section_acts.shape, bf16),
-            jax.ShapeDtypeStruct(section_grads.shape, bf16),
-            jax.ShapeDtypeStruct((1, tokens), f32),
+            pltpu.VMEM(section_acts.shape, bf16),
+            pltpu.VMEM(section_grads.shape, bf16),
+            pltpu.VMEM((1, tokens), f32),
         ),
         in_specs=[hbm, hbm, vmem, vmem, vmem, vmem, hbm, hbm, hbm, hbm],
-        out_specs=(hbm, hbm, vmem),
+        out_specs=(vmem, vmem, vmem),
         scratch_shapes=[pltpu.VMEM(shape, bf16) for shape in shapes]
         + [pltpu.VMEM(shape, f32) for shape in slots]
-        + [dma((3,)), dma((GROUP,)), dma((CHUNKS,))]
+        + [dma((3,))]
         + two(2)
         + two(2, experts - 1)
         + two(GROUP)

time: 155 us -> 152 us (0.981)
  the two profiles are of different devices: /device:TPU:264 before, /device:TPU:392 now
where the time goes in v5:
time: 152 us
  Pallas kernels  149 us (98%)
  local copies, waits for them, and re-layouts  2.05 us (1%)
    pallas_call x1, Pallas kernels, on_device(): pl.pallas_call(kernel, out_shape=(pltpu.VMEM(section_acts.shape, bf16), p...  149 us

profile of v5, /device:TPU:392, one launch (start us, length us, event | category | flops | bytes accessed | tf_op | source)
XLA Modules:
  0.0 152.0 jit_solution(10374995859146224604)
XLA Ops:
  0.6 149.3 %relay_experts.1 = (bf16[1,64,3584]{2,1,0:T(8,128)(2,1)S(1)}, bf16[1,64,3584]{2,1,0:T(8,128)(2,1)S(1)}, f32[1,64]{1,0:T(1,128)S(1)}) custom-call(bf16[1,64,3584]{2,1,0:T(8,128)(2,1)} %acts.1, bf16[1,64,3584]{2,1,0:T(8,128)(2,1)} %grads.1, s32[1,64]{1,0:T(1,128)} %bitcast.6, f32[1,64]{1,0:T(1,128)} %bitcast.7, s32[1,64]{1,0:T(1,128)} %bitcast.8, ...), custom_call_target="tpu_custom_call" | custom-call | flops 2818572288 | bytes 4587520 | tf_op jit(solution)/shard_map/relay_experts/pallas_call | solution.py:761
  150.0 0.8 copy.16
  150.8 0.5 copy.18
  151.3 0.8 copy.17

commit v6 on v5

--- a/solution.py
+++ b/solution.py
@@ -11,6 +11,7 @@
 CHUNKS = 4
 PAIRS = GROUP // 2
 LANES = 128
+HOLDERS = GROUP // 2
 HOPS = 4
 MESH = pl.DeviceIdType.MESH
 WAYS = ((0, 1), (1, -1))
@@ -60,14 +61,6 @@
     )
     unpack = jnp.where(named & (before == (slot % cap).astype(f32)), 1.0, 0.0).astype(bf16)
     return pack, unpack
-
-
-def slices_of(model):
-    tiles = model // LANES
-    wide, slim = -(-tiles // GROUP) * LANES, tiles // GROUP * LANES
-    many = tiles % GROUP
-    starts = [min(r, many) * wide + max(r - many, 0) * slim for r in range(GROUP)]
-    return [(start, wide if r < many else slim) for r, start in enumerate(starts)], many
 
 
 def kernel(
@@ -144,23 +137,17 @@
     experts, chunks, cap, width = packed_a.shape
     model, hidden = both_w.shape[0], both_w.shape[1] // 2
     spread = experts * cap
-    slices, many = slices_of(model)
-    wide, slim = slices[0][1], slices[-1][1]
-    shift = stage % 2 * many
-
-    def slice_at(yy):
-        return (yy + shift) % GROUP
-
-    mine = slice_at(y)
-
-    def with_slice(r, act):
-        @pl.when(r < many)
-        def _():
-            act(pl.multiple_of(r * wide, LANES), wide)
-
-        @pl.when(r >= many)
-        def _():
-            act(pl.multiple_of(many * wide + (r - many) * slim, LANES), slim)
+    size = model // HOLDERS
+    turn = stage % 2
+    holds = y % 2 == turn
+    passes = y % 2 != turn
+    mine = y // 2
+
+    def holder(r):
+        return 2 * r + turn
+
+    def at_y(yy):
+        return {"expert": x * GROUP + yy}
 
     def column(xx):
         return {"expert": xx * GROUP + y}
@@ -207,36 +194,40 @@
     for ab in (0, 1):
         pipe_copy(ab).start()
 
-    def deal_copy(j, start, size):
-        return remote(
-            w_down.at[0, 0, :, pl.ds(start, size)],
-            held.at[y, :, pl.ds(0, size)],
-            deal_send.at[j],
-            deal_recv.at[j],
-            ring(j),
-        )
-
-    def deal_own(start, size):
-        return pltpu.make_async_copy(
-            w_down.at[0, 0, :, pl.ds(start, size)], held.at[y, :, pl.ds(0, size)], deal_send.at[0]
-        )
-
-    def deal(j):
-        with_slice(slice_at(y + j), lambda start, size: deal_copy(j, start, size).start())
-
-    def deal_sent(j):
-        with_slice(slice_at(y + j), lambda start, size: deal_copy(j, start, size).wait_send())
-
-    def deal_got(start, size):
-        def body(j):
-            got = held.at[(y + GROUP - j) % GROUP, :, pl.ds(0, size)]
-            remote(got, got, deal_send.at[j], deal_recv.at[j], ring(j)).wait_recv()
-
-        deal_own(start, size).wait()
-        each(GROUP, body, 1)
-
-    each(GROUP, deal, 1)
-    with_slice(mine, lambda start, size: deal_own(start, size).start())
+    def to_holder(r, source, target, send, recv):
+        return remote(source, target.at[y], send.at[r], recv.at[y], at_y(holder(r)))
+
+    def to_self(r, source, target, send):
+        return pltpu.make_async_copy(source, target.at[y], send.at[r])
+
+    def hold_start(r, source, *rest):
+        pl.when(holder(r) != y)(lambda: to_holder(r, source, *rest).start())
+        pl.when(holder(r) == y)(lambda: to_self(r, source, *rest[:2]).start())
+
+    def hold_sent(r, source, *rest):
+        pl.when(holder(r) != y)(lambda: to_holder(r, source, *rest).wait_send())
+
+    def hold_own(r, source, *rest):
+        pl.when(holder(r) == y)(lambda: to_self(r, source, *rest[:2]).wait())
+
+    def hold_got(target, send, recv):
+        def body(g):
+            got = target.at[g]
+            pl.when(g != y)(
+                lambda: remote(got, got, send.at[0], recv.at[g], at_y(g)).wait_recv()
+            )
+
+        pl.when(holds)(lambda: each(GROUP, body))
+
+    def deal(r):
+        source = w_down.at[0, 0, :, pl.ds(r * size, size)]
+        return r, source, held, deal_send, deal_recv
+
+    def cot(r):
+        return r, local_b.at[:, r], cot_b, cot_send, cot_recv
+
+    for r in range(HOLDERS):
+        hold_start(*deal(r))
     loads = [
         pltpu.make_async_copy(w_gate.at[0, 0], both_w.at[:, pl.ds(0, hidden)], load_sem.at[0]),
         pltpu.make_async_copy(w_up.at[0, 0], both_w.at[:, pl.ds(hidden, hidden)], load_sem.at[1]),
@@ -245,10 +236,9 @@
     for load in loads:
         load.start()
 
-    @pl.when(mine >= many)
+    @pl.when(passes)
     def _():
-        held[:, :, slim:] = jnp.zeros((GROUP, hidden, wide - slim), bf16)
-        cot_b[:, :, :, slim:] = jnp.zeros((GROUP, experts, cap, wide - slim), bf16)
+        dhid_part[y] = jnp.zeros(dhid_part.shape[1:], bf16)
 
     pack_a, unpack_a = place_matrices(routes_a[...], experts, cap)
     pack_b, unpack_b = place_matrices(routes_b[...], experts, cap)
@@ -284,42 +274,11 @@
         spread_copy(0, j).start()
     rows_a[y, :, x] = packed_a[x]
     pipe_copy(1).wait_recv()
-    packed_b[:, many:, :, slim:] = jnp.zeros((experts, GROUP - many, cap, wide - slim), bf16)
-    for r, (start, size) in enumerate(slices):
-        packed_b[:, r, :, :size] = packed_rows(pack_b, in_b, start, size)
+    for r in range(HOLDERS):
+        packed_b[:, r] = packed_rows(pack_b, in_b, r * size, size)
     for j in range(1, experts):
         spread_copy(1, j).start()
     local_b[x] = packed_b[x]
-
-    def cot_copy(j, size):
-        return remote(
-            local_b.at[:, slice_at(y + j), :, pl.ds(0, size)],
-            cot_b.at[y, :, :, pl.ds(0, size)],
-            cot_send.at[j],
-            cot_recv.at[j],
-            ring(j),
-        )
-
-    def cot_own(size):
-        return pltpu.make_async_copy(
-            local_b.at[:, mine, :, pl.ds(0, size)],
-            cot_b.at[y, :, :, pl.ds(0, size)],
-            cot_send.at[0],
-        )
-
-    def cot_got(start, size):
-        def body(j):
-            got = cot_b.at[(y + GROUP - j) % GROUP, :, :, pl.ds(0, size)]
-            remote(got, got, cot_send.at[j], cot_recv.at[j], ring(j)).wait_recv()
-
-        cot_own(size).wait()
-        each(GROUP, body, 1)
-
-    def cot(j):
-        with_slice(slice_at(y + j), lambda start, size: cot_copy(j, size).start())
-
-    def cot_sent(j):
-        with_slice(slice_at(y + j), lambda start, size: cot_copy(j, size).wait_send())
 
     def halves(ref, d, t, far):
         half = ref.shape[0] // 2
@@ -330,9 +289,9 @@
             self.blocks, self.send, self.recv = blocks, send, recv
             self.count = blocks.shape[1]
 
-        def copy(self, t, c, d, sign, on=0):
+        def copy(self, t, c, d, sign, on=0, part=False):
             at = self.blocks.at[(y + GROUP - sign * (t + on)) % GROUP, c]
-            at = halves(at, d, t, HOPS - 1)
+            at = halves(at, d, t, t if part else HOPS - 1)
             k = t * self.count + c
             return remote(at, at, self.send.at[d, k], self.recv.at[d, k], ring(sign))
 
@@ -350,6 +309,39 @@
             for t in range(HOPS):
                 for d, sign in WAYS:
                     self.copy(t, c, d, sign).wait_send()
+
+    class HolderGather(Gather):
+        def step(self, t, c):
+            for d, sign in WAYS:
+                if t == 1 or t == 2:
+                    self.copy(t - 1, c, d, sign, 1).wait_recv()
+                if t < 2:
+                    self.copy(t, c, d, sign).start()
+                elif t == 2:
+                    pl.when(holds)(lambda: self.copy(2, c, d, sign, 0, True).start())
+                    pl.when(passes)(lambda: self.copy(2, c, d, sign).start())
+                else:
+                    pl.when(holds)(lambda: self.copy(2, c, d, sign, 1).wait_recv())
+
+                    @pl.when(passes)
+                    def _():
+                        self.copy(2, c, d, sign, 1, True).wait_recv()
+                        self.copy(3, c, d, sign, 0, True).start()
+
+        def last(self, c):
+            for d, sign in WAYS:
+                pl.when(holds)(lambda: self.copy(3, c, d, sign, 1, True).wait_recv())
+
+        def sent(self, c):
+            for d, sign in WAYS:
+                for t in (0, 1):
+                    self.copy(t, c, d, sign).wait_send()
+                pl.when(holds)(lambda: self.copy(2, c, d, sign, 0, True).wait_send())
+
+                @pl.when(passes)
+                def _():
+                    self.copy(2, c, d, sign).wait_send()
+                    self.copy(3, c, d, sign, 0, True).wait_send()
 
     class Fold:
         def __init__(self, part, sums, send, recv):
@@ -397,14 +389,63 @@
                 for d, sign in WAYS:
                     self.copy(t, c, d, sign).wait_send()
 
+    class HolderFold(Fold):
+        def onward(self, t, c, d, sign, part=False, at=None):
+            k = t * self.count + c
+            source = self.sums.at[d, t if at is None else at, c]
+            target = self.sums.at[d, t, c]
+            return remote(
+                halves(source, d, t, t if part else HOPS),
+                halves(target, d, t, t if part else HOPS),
+                self.send.at[d, k],
+                self.recv.at[d, k],
+                ring(sign),
+            )
+
+        def step(self, t, c):
+            half = self.part.shape[2] // 2
+            for d, sign in WAYS:
+
+                @pl.when(holds)
+                def _():
+                    if t >= 2:
+                        self.onward(t - 1, c, d, sign, t == 2).wait_recv()
+                        block = (y + GROUP + sign * (HOPS - t)) % GROUP
+                        at = pl.ds(d * half, half) if t == 2 else pl.ds(0, 2 * half)
+                        self.part[block, c, at] = (
+                            self.part[block, c, at].astype(f32)
+                            + self.sums[d, t - 1, c, at].astype(f32)
+                        ).astype(bf16)
+                    self.copy(t, c, d, sign).start()
+
+                if t:
+
+                    @pl.when(passes)
+                    def _():
+                        self.onward(t - 1, c, d, sign, t == 1).wait_recv()
+                        self.onward(t, c, d, sign, t == 1, t - 1).start()
+
+        def sent(self, c):
+            for d, sign in WAYS:
+
+                @pl.when(holds)
+                def _():
+                    for t in range(HOPS):
+                        self.copy(t, c, d, sign).wait_send()
+
+                @pl.when(passes)
+                def _():
+                    for t in range(1, HOPS):
+                        self.onward(t, c, d, sign, t == 1, t - 1).wait_send()
+
     rows = Gather(rows_a, rows_send, rows_recv)
-    hids = Gather(hid_all, hid_send, hid_recv)
-    dhids = Fold(dhid_part, dhid_sums, dhid_send, dhid_recv)
+    hids = HolderGather(hid_all, hid_send, hid_recv)
+    dhids = HolderFold(dhid_part, dhid_sums, dhid_send, dhid_recv)
     grads_x = Fold(part_b, sums_b, fold_send, fold_recv)
 
     def dhid_partial(p):
-        here = cot_b[pl.ds(2 * p, 2)].reshape(2 * spread, wide)
-        dhid = nt_dot(here, held[...].reshape(GROUP * hidden, wide)).astype(bf16)
+        here = cot_b[pl.ds(2 * p, 2)].reshape(2 * spread, size)
+        dhid = nt_dot(here, held[...].reshape(GROUP * hidden, size)).astype(bf16)
         for g in range(GROUP):
             dhid_part[g, p] = dhid[:, g * hidden : (g + 1) * hidden].reshape(2, spread, hidden)
 
@@ -425,9 +466,9 @@
             [hid_all[g, p].reshape(2 * spread, hidden) for g in range(GROUP)], axis=1
         )
         done = jnp.dot(
-            hid, held[...].reshape(GROUP * hidden, wide), preferred_element_type=f32
-        )
-        slice_part[pl.ds(2 * p, 2)] = done.astype(bf16).reshape(2, experts, cap, wide)
+            hid, held[...].reshape(GROUP * hidden, size), preferred_element_type=f32
+        )
+        slice_part[pl.ds(2 * p, 2)] = done.astype(bf16).reshape(2, experts, cap, size)
 
     def backward(p):
         dhid = dhids.total(p).reshape(2 * spread, hidden)
@@ -450,49 +491,46 @@
                 .reshape(2, experts, cap, width)
             )
 
-    def slice_copy(j, size):
+    def slice_copy(b):
         return remote(
-            slice_part.at[(y + j) % GROUP, :, :, pl.ds(0, size)],
-            slice_got.at[mine, :, :, pl.ds(0, size)],
-            slice_send.at[j],
-            slice_recv.at[j],
-            ring(j),
-        )
+            slice_part.at[b], slice_got.at[mine], slice_send.at[b], slice_recv.at[mine], at_y(b)
+        )
+
+    def slice_out(p):
+        forward_out(p)
+        for b in (2 * p, 2 * p + 1):
+            pl.when(b != y)(lambda: slice_copy(b).start())
 
     def home_a_copy(r, j):
         to = (x + j) % experts
-        at = pl.ds(0, slices[r][1])
         return remote(
-            slice_got.at[r, to, :, at],
-            back_a.at[r, x, :, at],
+            slice_got.at[r, to],
+            back_a.at[r, x],
             home_a_send.at[r, j - 1],
             home_a_recv.at[r, j - 1],
             column(to),
         )
 
     def home_a(r):
-        off = (y + GROUP - (r + GROUP - shift) % GROUP) % GROUP
-
-        @pl.when(off != 0)
+        @pl.when(holder(r) != y)
         def _():
-            got = slice_got.at[r, :, :, pl.ds(0, slices[r][1])]
-            remote(got, got, slice_send.at[off], slice_recv.at[off], ring(1)).wait_recv()
+            got = slice_got.at[r]
+            remote(got, got, slice_send.at[0], slice_recv.at[r], ring(1)).wait_recv()
 
         for j in range(1, experts):
             home_a_copy(r, j).start()
         back_a[r, x] = slice_got[r, x]
 
     def finish_a(r):
-        start, size = slices[r]
         for j in range(1, experts):
-            got = back_a.at[r, (x + experts - j) % experts, :, pl.ds(0, size)]
+            got = back_a.at[r, (x + experts - j) % experts]
             remote(
                 got, got, home_a_send.at[r, j - 1], home_a_recv.at[r, j - 1], column(x)
             ).wait_recv()
         picked = jnp.dot(
-            unpack_a, back_a[r, :, :, :size].reshape(spread, size), preferred_element_type=f32
-        )
-        at = slice(start, start + size)
+            unpack_a, back_a[r].reshape(spread, size), preferred_element_type=f32
+        )
+        at = slice(r * size, (r + 1) * size)
         out_a[0, :, at] = (in_a[:, at].astype(f32) + gate_a * picked).astype(bf16)
 
     def straight_copy(c, d, j, sign, block):
@@ -531,7 +569,7 @@
         remote(
             got, got, straight_send.at[c, 0, 0], straight_recv.at[c], column(x)
         ).wait_recv()
-        picked = jnp.zeros((spread, width), f32)
+        picked = jnp.zeros((in_b.shape[0], width), f32)
         for d in range(3):
             rows_d = straight[c, d].reshape(spread, width)
             picked += jnp.dot(unpack_b, rows_d, preferred_element_type=f32)
@@ -600,8 +638,8 @@
     for t in range(HOPS):
         each(chunks, functools.partial(rows.step, t))
     spread_wait(1)
-    each(GROUP, cot, 1)
-    with_slice(mine, lambda start, size: cot_own(size).start())
+    for r in range(HOLDERS):
+        hold_start(*cot(r))
     for load in loads:
         load.wait()
     each(chunks, rows.last)
@@ -611,11 +649,14 @@
         hids.step(0, p)
 
     each(PAIRS, body)
-    with_slice(mine, deal_got)
-    with_slice(mine, cot_got)
+    for r in range(HOLDERS):
+        hold_own(*deal(r))
+        hold_own(*cot(r))
+    hold_got(held, deal_send, deal_recv)
+    hold_got(cot_b, cot_send, cot_recv)
 
     def body(p):
-        dhid_partial(p)
+        pl.when(holds)(lambda: dhid_partial(p))
         dhids.step(0, p)
         hids.step(1, p)
 
@@ -636,15 +677,13 @@
     def body(p):
         dhids.step(3, p)
         hids.last(p)
-        forward_out(p)
-        for i in (0, 1):
-            j = (2 * p + i + GROUP - y) % GROUP
-            pl.when(j != 0)(
-                lambda: with_slice(mine, lambda start, size: slice_copy(j, size).start())
-            )
+        pl.when(holds)(lambda: slice_out(p))
 
     each(PAIRS, body)
-    slice_got[mine] = slice_part[y]
+
+    @pl.when(holds)
+    def _():
+        slice_got[mine] = slice_part[y]
 
     backward((y // 2 + PAIRS // 2) % PAIRS)
     each(chunks, lambda c: grads_x.step(0, c))
@@ -655,33 +694,34 @@
     each(chunks, straight_mine)
     each(chunks, lambda c: grads_x.step(1, c))
     slot_step(1)
-    for r in range(GROUP):
+    for r in range(HOLDERS):
         home_a(r)
     each(chunks, lambda c: grads_x.step(2, c))
     slot_step(2)
     each(chunks, lambda c: grads_x.step(3, c, straight_last))
     slot_step(3)
-    for r in range(GROUP):
+    for r in range(HOLDERS):
         finish_a(r)
 
     for ab in (0, 1):
         pipe_copy(ab).wait_send()
         for j in range(1, experts):
             spread_copy(ab, j).wait_send()
-    each(GROUP, deal_sent, 1)
-    each(GROUP, cot_sent, 1)
+    for r in range(HOLDERS):
+        hold_sent(*deal(r))
+        hold_sent(*cot(r))
     each(chunks, rows.sent)
     each(PAIRS, dhids.sent)
     each(PAIRS, hids.sent)
 
-    def body(start, size):
-        each(GROUP, lambda j: slice_copy(j, size).wait_send(), 1)
-
-    with_slice(mine, body)
+    def body(b):
+        pl.when(b != y)(lambda: slice_copy(b).wait_send())
+
+    pl.when(holds)(lambda: each(GROUP, body))
 
     slot_last()
 
-    for r in range(GROUP):
+    for r in range(HOLDERS):
         for j in range(1, experts):
             home_a_copy(r, j).wait_send()
     each(chunks, lambda c: grads_x.sent(c, HOPS - 1))
@@ -718,9 +758,9 @@
     sources = saved_proj.shape[1]
     spread = experts * cap
     lanes = 2 * spread
-    wide = slices_of(model)[0][0][1]
+    size = model // HOLDERS
     whole = (tokens, model)
-    by_slice = (experts, GROUP, cap, wide)
+    by_slice = (experts, HOLDERS, cap, size)
     by_chunk = (experts, CHUNKS, cap, width)
     blocks = (CHUNKS, experts, cap, width)
     hids = (PAIRS, 2, spread, hidden)
@@ -741,16 +781,16 @@
         by_slice,
         (GROUP,) + blocks,
         by_slice,
-        (GROUP, experts, cap, wide),
-        (GROUP, hidden, wide),
+        (GROUP, experts, cap, size),
+        (GROUP, hidden, size),
         (GROUP,) + hids,
         (2, HOPS) + hids,
         (GROUP,) + hids,
-        (GROUP, experts, cap, wide),
-        (GROUP, experts, cap, wide),
+        (GROUP, experts, cap, size),
+        (HOLDERS, experts, cap, size),
         (GROUP,) + blocks,
         (2, HOPS) + blocks,
-        (GROUP, experts, cap, wide),
+        (HOLDERS, experts, cap, size),
         (CHUNKS, 3, experts, cap, width),
         (model, 2 * hidden),
         (sources, cap, 2 * hidden),
@@ -772,13 +812,12 @@
         + [dma((3,))]
         + two(2)
         + two(2, experts - 1)
-        + two(GROUP)
-        + two(GROUP)
+        + [dma((HOLDERS,)), dma((GROUP,))] * 2
         + two(2, HOPS * CHUNKS)
         + two(2, HOPS * PAIRS)
         + two(2, HOPS * PAIRS)
-        + two(GROUP)
-        + two(GROUP, experts - 1)
+        + [dma((GROUP,)), dma((HOLDERS,))]
+        + two(HOLDERS, experts - 1)
         + two(2, HOPS * CHUNKS)
         + [dma((CHUNKS, 3, experts)), dma((CHUNKS,))]
         + two(2, HOPS)

time: 152 us -> 151 us (level)
  the two profiles are of different devices: /device:TPU:392 before, /device:TPU:8 now
where the time goes in v6:
time: 151 us
  Pallas kernels  149 us (99%)
  local copies, waits for them, and re-layouts  2.05 us (1%)
    pallas_call x1, Pallas kernels, on_device(): pl.pallas_call(kernel, out_shape=(pltpu.VMEM(section_acts.shape, bf16), p...  149 us

profile of v6, /device:TPU:8, one launch (start us, length us, event | category | flops | bytes accessed | tf_op | source)
XLA Modules:
  0.0 151.2 jit_solution(17844200806335691650)
XLA Ops:
  0.6 148.5 %relay_experts.1 = (bf16[1,64,3584]{2,1,0:T(8,128)(2,1)S(1)}, bf16[1,64,3584]{2,1,0:T(8,128)(2,1)S(1)}, f32[1,64]{1,0:T(1,128)S(1)}) custom-call(bf16[1,64,3584]{2,1,0:T(8,128)(2,1)} %acts.1, bf16[1,64,3584]{2,1,0:T(8,128)(2,1)} %grads.1, s32[1,64]{1,0:T(1,128)} %bitcast.6, f32[1,64]{1,0:T(1,128)} %bitcast.7, s32[1,64]{1,0:T(1,128)} %bitcast.8, ...), custom_call_target="tpu_custom_call" | custom-call | flops 2818572288 | bytes 4587520 | tf_op jit(solution)/shard_map/relay_experts/pallas_call | solution.py:801
  149.1 0.8 copy.16
  149.9 0.5 copy.18
  150.4 0.8 copy.17

commit v7 on v6

--- a/solution.py
+++ b/solution.py
@@ -74,8 +74,7 @@
     w_gate,
     w_up,
     w_down,
-    out_a,
-    out_b,
+    results,
     out_g,
     in_a,
     in_b,
@@ -531,7 +530,7 @@
             unpack_a, back_a[r].reshape(spread, size), preferred_element_type=f32
         )
         at = slice(r * size, (r + 1) * size)
-        out_a[0, :, at] = (in_a[:, at].astype(f32) + gate_a * picked).astype(bf16)
+        results[0, :, at] = (in_a[:, at].astype(f32) + gate_a * picked).astype(bf16)
 
     def straight_copy(c, d, j, sign, block):
         return remote(
@@ -573,7 +572,7 @@
         for d in range(3):
             rows_d = straight[c, d].reshape(spread, width)
             picked += jnp.dot(unpack_b, rows_d, preferred_element_type=f32)
-        out_b[0, :, columns(c)] = (in_b[:, columns(c)].astype(f32) + gate_b * picked).astype(bf16)
+        results[1, :, columns(c)] = (in_b[:, columns(c)].astype(f32) + gate_b * picked).astype(bf16)
 
     def slot_copy(d, t, sign):
         return remote(
@@ -798,15 +797,14 @@
     slots = [(PAIRS, 8, lanes), (2, HOPS, 8, lanes), (2, HOPS, 8, lanes), (8, lanes)]
     slots.append((experts, 8, lanes))
 
-    out_a, out_b, out_g = pl.pallas_call(
+    results, out_g = pl.pallas_call(
         kernel,
         out_shape=(
-            pltpu.VMEM(section_acts.shape, bf16),
-            pltpu.VMEM(section_grads.shape, bf16),
+            pltpu.VMEM((2, tokens, model), bf16),
             pltpu.VMEM((1, tokens), f32),
         ),
         in_specs=[hbm, hbm, vmem, vmem, vmem, vmem, hbm, hbm, hbm, hbm],
-        out_specs=(vmem, vmem, vmem),
+        out_specs=(vmem, vmem),
         scratch_shapes=[pltpu.VMEM(shape, bf16) for shape in shapes]
         + [pltpu.VMEM(shape, f32) for shape in slots]
         + [dma((3,))]
@@ -843,7 +841,7 @@
         w_up,
         w_down,
     )
-    return out_a, out_b, out_g.reshape(1, tokens, 1)
+    return results[:1], results[1:], out_g.reshape(1, tokens, 1)
 
 
 def solution(mesh):

time: 151 us -> 151 us (level)
    unnamed x3 -> x1, local copies, waits for them, and re-layouts: 2.05 us -> 0.51 us
where the time goes in v7:
time: 151 us
  Pallas kernels  149 us (99%)
    pallas_call x1, Pallas kernels, on_device(): pl.pallas_call(kernel, out_shape=(pltpu.VMEM((2, tokens, model), bf16), p...  149 us

profile of v7, /device:TPU:8, one launch (start us, length us, event | category | flops | bytes accessed | tf_op | source)
XLA Modules:
  0.0 150.6 jit_solution(16320636867538803733)
XLA Ops:
  0.6 148.5 %relay_experts.1 = (bf16[2,64,3584]{2,1,0:T(8,128)(2,1)S(1)}, f32[1,64]{1,0:T(1,128)S(1)}) custom-call(bf16[1,64,3584]{2,1,0:T(8,128)(2,1)} %acts.1, bf16[1,64,3584]{2,1,0:T(8,128)(2,1)} %grads.1, s32[1,64]{1,0:T(1,128)} %bitcast.6, f32[1,64]{1,0:T(1,128)} %bitcast.7, s32[1,64]{1,0:T(1,128)} %bitcast.8, f32[1,64]{1,0:T(1,128)} %bitcast.9, ...), custom_call_target="tpu_custom_call" | custom-call | flops 2818572288 | bytes 4587520 | tf_op jit(solution)/shard_map/relay_experts/pallas_call | solution.py:800
  149.2 0.5 copy.14
  149.7 1.0 fusion
